TPU v7x, 128 devices: a whole 4x4x4 slice. The times are simulated.
128 devices in a mesh: section: 4 (over z), seq: 32 (over x, y, core).
Axes of the slice: x: 4, y: 4, z: 4, core: 2. Of those that a mesh axis runs over, the one named last changes fastest.
Arguments:
- projected: bfloat16 [4, 3, 16384, 3072], P('section', None, 'seq'), may hold values from -24 to 24
- gate: bfloat16 [4, 3072], P('section'), may hold values from 2 to 8
- head_class: int32 [24], replicated, may hold values 0 or 1
- tile_lists: int32 [2, 128, 8], replicated, may hold values from 0 to 127, as said below
- tile_counts: int32 [24, 128], replicated, may hold values from 1 to 8, as said below
Outputs:
- next_input: bfloat16 [4, 16384, 3072], P('section', 'seq')
Inputs may be any that keep to these rules, and one draw needn't show every extreme that they name: tile_lists[c, t, 0] = t, and the 8 entries of a row are distinct tiles. `tile_counts`: counts differ strongly from head to head.
All inputs are finite; a program needn't handle non-finite values.
Results may differ from a plain program's by a relative error of at most 0.0057.
Values may be sent and summed in bfloat16 or wider, within the bound.
No kernel may reach another device: no remote copies, remote signals or barrier semaphores. Data moves between devices by JAX's collectives and lax.ppermute only.
A program may use at most 128 MiB of HBM per device.

v0:
```python
import jax
import jax.numpy as jnp
from jax import lax
from jax.sharding import PartitionSpec as P

H = 24
HD = 128
QG = 8


def from_behind(block, axis, distance):
    devices = range(lax.axis_size(axis))
    route = [((i - distance) % len(devices), i) for i in devices]
    return lax.ppermute(block, axis, route)


def attend_tiles(query_tiles, key_tiles, value_tiles, tile_rows, counts):
    ntiles = tile_rows.shape[0]
    kmax = tile_rows.shape[1]
    tile_len = query_tiles.shape[1]
    depth = query_tiles.shape[2]
    scale_factor = depth ** (-0.5)

    def one_group(group):
        offset = group * QG
        group_queries = lax.dynamic_slice_in_dim(query_tiles, offset, QG, 0)
        group_rows = lax.dynamic_slice_in_dim(tile_rows, offset, QG, 0)
        group_counts = lax.dynamic_slice_in_dim(counts, offset, QG, 0)
        gathered_keys = key_tiles[group_rows].reshape(QG, kmax * tile_len, depth)
        gathered_values = value_tiles[group_rows].reshape(QG, kmax * tile_len, depth)
        scores = (
            jnp.einsum(
                "qtd,qkd->qtk", group_queries, gathered_keys, preferred_element_type=jnp.float32
            )
            * scale_factor
        )
        usable = jnp.arange(kmax, dtype=jnp.int32)[None, :] < group_counts[:, None]
        usable = jnp.repeat(usable, tile_len, axis=1)[:, None, :]
        scores = jnp.where(usable, scores, -jnp.inf)
        highest = jnp.max(scores, axis=-1, keepdims=True)
        raised = jnp.exp(scores - highest)
        weights = (raised / jnp.sum(raised, axis=-1, keepdims=True)).astype(jnp.bfloat16)
        mixed = jnp.einsum(
            "qtk,qkd->qtd", weights, gathered_values, preferred_element_type=jnp.float32
        )
        return mixed.astype(jnp.bfloat16)

    grouped = lax.map(one_group, jnp.arange(ntiles // QG, dtype=jnp.int32))
    return grouped.reshape(ntiles, tile_len, depth)


def attend_member(member, tile_rows, counts):
    ntiles = tile_rows.shape[0]
    local_rows = member.shape[1]
    tiles = member.reshape(3, ntiles, local_rows // ntiles, member.shape[2])
    full_out = attend_tiles(tiles[0], tiles[1], tiles[2], tile_rows, counts)
    return full_out.reshape(local_rows, member.shape[2])


def local(projected, gate, head_class, tile_lists, tile_counts):
    owners = lax.axis_size("seq")
    rank_here = lax.axis_index("seq")
    local_len = projected.shape[2]
    model_width = projected.shape[3]
    slot_count = -(-H // owners)
    spare = slot_count * owners - H
    heads_here = projected[0].reshape(3, local_len, H, HD)
    spread = jnp.pad(heads_here, ((0, 0), (0, 0), (0, spare), (0, 0)))
    spread = spread.reshape(3, local_len, slot_count, owners, HD).transpose(3, 2, 0, 1, 4)
    arrived = lax.all_to_all(spread, "seq", split_axis=0, concat_axis=3, tiled=True)
    head_id = 0 + rank_here
    member = arrived[0, 0]
    present = head_id < H
    source = jnp.minimum(head_id, H - 1)
    head_kind = lax.dynamic_index_in_dim(head_class, source, 0, keepdims=False)
    tile_rows = lax.dynamic_index_in_dim(tile_lists, head_kind, 0, keepdims=False)
    counts = lax.dynamic_index_in_dim(tile_counts, source, 0, keepdims=False)
    attended = attend_member(member, tile_rows, counts)
    gate_part = lax.dynamic_slice_in_dim(gate[0], source * HD, HD)
    attended = (gate_part.astype(jnp.float32)[None, :] * attended.astype(jnp.float32)).astype(
        jnp.bfloat16
    )
    results = [jnp.where(present, attended, jnp.zeros_like(attended))]
    stacked = jnp.stack(results).reshape(slot_count, owners, local_len, HD)
    shifted = from_behind(stacked, "section", 1)
    returned = lax.all_to_all(shifted, "seq", split_axis=1, concat_axis=1, tiled=True)
    rows = returned.transpose(2, 0, 1, 3).reshape(local_len, slot_count * owners, HD)
    return rows[:, :H].reshape(local_len, model_width)[None]


def solution(mesh):
    placed = (P("section", None, "seq", None), P("section", None), P(), P(), P())
    return jax.shard_map(
        local, mesh=mesh, in_specs=placed, out_specs=P("section", "seq", None), check_vma=False
    )
```

profile of v0, /device:TPU:1, one launch (start us, length us, event | category | flops | bytes accessed | tf_op | source)
XLA Modules:
  0.0 686.0 jit_solution(2301099276002126212)
XLA Ops:
  0.0 12.7 %copy.10 = bf16[1,3,512,3072]{2,3,1,0:T(8,128)(2,1)} copy(bf16[1,3,512,3072]{3,2,1,0:T(8,128)(2,1)} %param.7) | data formatting | bytes 18874368 | tf_op args[0]
  12.7 9.5 %pad_bitcast_fusion = bf16[32,1,3,512,128]{3,4,0,2,1:T(8,128)(2,1)} fusion(bf16[3,512,24,128]{1,3,2,0:T(8,128)(2,1)} %bitcast.55), kind=kLoop, calls=%fused_computation.23 | loop fusion | bytes 22020096 | tf_op jit(solution)/shard_map/transpose | solution.py:69
  22.2 16.7 %copy.11 = bf16[32,1,3,512,128]{4,3,2,1,0:T(8,128)(2,1)} copy(bf16[32,1,3,512,128]{3,4,0,2,1:T(8,128)(2,1)} %pad_bitcast_fusion) | data formatting | bytes 25165824 | tf_op jit(solution)/shard_map/transpose | solution.py:69
  38.9 8.8 %all-to-all-start = ((bf16[32,1,3,512,128]{4,3,2,1,0:T(8,128)(2,1)}), bf16[32,1,3,512,128]{4,3,2,1,0:T(8,128)(2,1)}, u32[]{:S(2)}, u32[]{:S(2)}) async-start(bf16[32,1,3,512,128]{4,3,2,1,0:T(8,128)(2,1)} %copy.11), calls=%async_computation | async-start | bytes 25165824 | tf_op jit(solution)/shard_map/all_to_all | solution.py:70
  51.0 171.3 %all-to-all-done = bf16[32,1,3,512,128]{4,3,2,1,0:T(8,128)(2,1)} async-done(((bf16[32,1,3,512,128]{4,3,2,1,0:T(8,128)(2,1)}), bf16[32,1,3,512,128]{4,3,2,1,0:T(8,128)(2,1)}, u32[]{:S(2)}, u32[]{:S(2)}) %all-to-all-start) | async-done | bytes 12582944 | tf_op jit(solution)/shard_map/all_to_all | solution.py:70
  222.3 8.9 %fusion.20 = (bf16[1,1,1,32,512,128]{5,4,2,3,1,0:T(8,128)(2,1)}, bf16[1,1,1,32,512,128]{5,4,2,3,1,0:T(8,128)(2,1)}, bf16[1,1,1,32,512,128]{5,4,2,3,1,0:T(8,128)(2,1)}) fusion(bf16[1,1,3,32,512,128]{5,4,2,3,1,0:T(8,128)(2,1)} %bitcast.11), kind=kLoop, calls=%fused_computation.34 | loop fusion | bytes 25165824 | tf_op jit(solution)/shard_map/slice | solution.py:56
  231.2 265.0 %while.10 = (s32[]{:T(128)}, bf16[16,8,128,128]{3,2,1,0:T(8,128)(2,1)}, s32[16]{0:T(128)S(1)}, s32[128]{0:T(128)S(1)}, bf16[128,128,128]{2,1,0:T(8,128)(2,1)}, /...) while((s32[]{:T(128)}, ...), condition=%wide.region_3.4_spmd, body=%wide.region_0.3_spmd.sunk | while | flops 545392896 | bytes 29915804 | solution.py:48
  244.0 3.8 fusion.34
  260.6 3.8 fusion.34
  277.2 3.8 fusion.34
  293.7 3.8 fusion.34
  310.3 3.8 fusion.34
  343.4 3.8 fusion.34
  360.0 3.8 fusion.34
  393.1 3.8 fusion.34
  409.6 3.8 fusion.34
  426.2 3.8 fusion.34
  442.7 3.8 fusion.34
  459.3 3.8 fusion.34
  475.8 3.8 fusion.34
  492.4 3.8 fusion.34
  501.3 91.2 %collective-permute-done = bf16[1,32,512,128]{3,2,0,1:T(8,128)(2,1)S(1)} collective-permute-done((bf16[1,32,512,128]{3,2,0,1:T(8,128)(2,1)S(1)}, bf16[1,32,512,128]{3,2,0,1:T(8,128)(2,1)S(1)}, u32[]{:S(2)}, u32[]{:S(2)}) %collective-permute-start) | collective-permute-done | bytes 4194336 | tf_op jit(solution)/shard_map/ppermute | solution.py:14
  592.6 81.7 %all_to_all.20 = bf16[1,32,512,128]{3,2,0,1:T(8,128)(2,1)} all-to-all(bf16[1,32,512,128]{3,2,0,1:T(8,128)(2,1)S(1)} %collective-permute-done), channel_id=1, replica_groups=mesh['section'=4,'seq'=32] {'seq'}, dimensions={1} | all-to-all | bytes 8388608 | tf_op jit(solution)/shard_map/all_to_all | solution.py:86
  674.2 6.5 copy.13
  (197 shorter events, 213.2 us)
Async XLA Ops:
  0.0 50.3 %copy-start = (s32[24,128]{1,0:T(8,128)S(1)}, s32[24,128]{1,0:T(8,128)}, u32[]{:S(2)}) copy-start(s32[24,128]{1,0:T(8,128)} %param.11) | copy-start | bytes 36868
  38.9 8.8 %copy-start.3 = (s32[24]{0:T(128)S(1)}, s32[24]{0:T(128)}, u32[]{:S(2)}) copy-start(s32[24]{0:T(128)} %param.9) | copy-start | bytes 292
  38.9 11.3 %copy-start.2 = (s32[2,128,8]{1,2,0:T(8,128)S(1)}, s32[2,128,8]{1,2,0:T(8,128)}, u32[]{:S(2)}) copy-start(s32[2,128,8]{1,2,0:T(8,128)} %param.10) | copy-start | bytes 24580
  38.9 183.4 %all-to-all-start = ((bf16[32,1,3,512,128]{4,3,2,1,0:T(8,128)(2,1)}), bf16[32,1,3,512,128]{4,3,2,1,0:T(8,128)(2,1)}, u32[]{:S(2)}, u32[]{:S(2)}) async-start(bf16[32,1,3,512,128]{4,3,2,1,0:T(8,128)(2,1)} %copy.11), calls=%async_computation | async-start | bytes 25165824 | tf_op jit(solution)/shard_map/all_to_all | solution.py:70
  499.6 92.9 %collective-permute-start = (bf16[1,32,512,128]{3,2,0,1:T(8,128)(2,1)S(1)}, bf16[1,32,512,128]{3,2,0,1:T(8,128)(2,1)S(1)}, u32[]{:S(2)}, u32[]{:S(2)}) collective-permute-start(bf16[1,32,512,128]{3,2,0,1:T(8,128)(2,1)S(1)} %fusion.15), channel_id=1, source_target_pairs={{96,0},{0,32},{32,64},{64,96},{97,1},{1,33},{33,65},{65,97},{98,2}... | collective-permute-start | bytes 12582920 | tf_op jit(solution)/shard_map/ppermute | solution.py:14
  680.7 5.2 copy-start.1
where the time goes:
time: 690 us; the launch traced here: 686 us
  waiting for transfers between devices  263 us (38%)
  local copies, waits for them, and re-layouts  174 us (25%)
  matrix products  87.2 us (13%)
  blocking collectives  81.7 us (12%)
  other arithmetic  57.6 us (8%)
  loops' own time  10.6 us (2%)
  starting transfers between devices  10.5 us (2%)
    all_to_all x1, waiting for transfers between devices, local(): lax.all_to_all(spread, 'seq', split_axis=0, concat_axis=3, tiled=True)  171 us
    ppermute x1, waiting for transfers between devices, from_behind(): return lax.ppermute(block, axis, route)  91.2 us
    all_to_all x1, blocking collectives, local(): lax.all_to_all(shifted, 'seq', split_axis=1, concat_axis=1, tiled=True)  81.7 us
    dot_general x16, matrix products, one_group(): jnp.einsum('qtk,qkd->qtd', weights, gathered_values, preferred_element_ty...  60.5 us
    sub x16, other arithmetic, one_group(): raised = jnp.exp(scores - highest)  53.1 us
    gather x16, local copies, waits for them, and re-layouts, one_group(): gathered_keys = key_tiles[group_rows].reshape(QG, kmax * tile_len, depth)  50.2 us
    gather x16, local copies, waits for them, and re-layouts, one_group(): value_tiles[group_rows].reshape(QG, kmax * tile_len, depth)  50.2 us
    dot_general x16, matrix products, one_group(): jnp.einsum('qtd,qkd->qtk', group_queries, gathered_keys, preferred_elemen...  26.7 us
  transfers between devices with their start and end apart: 2, of which 2 were waited for; matrix products, arithmetic and copies ran while one was open for 0% of the time, Pallas kernels for 0%

commit v1 on v0

v1 whole, which is shorter than its diff:
```python
import jax
import jax.numpy as jnp
from jax import lax
from jax.experimental import pallas as pl
from jax.experimental.pallas import tpu as pltpu
from jax.sharding import PartitionSpec as P

H = 24
HD = 128
TILE = 128
KMAX = 8
SHARED = 8
PAIRS = 8
CHIPS = 16
SLOTS = 2 * CHIPS
LOG2E = 1.4426950408889634


def pack_kernel(counts_ref, x_ref, out_ref, slot_ref, used_ref, sems):
    loads = jnp.sum(counts_ref[...].astype(jnp.float32), axis=1, keepdims=True)
    order = lax.broadcasted_iota(jnp.int32, (H, 1), 0).astype(jnp.float32)
    keys = loads * 32.0 + (31.0 - order)

    def clear(h, carry):
        used_ref[h] = 0
        return carry

    lax.fori_loop(0, H, clear, 0)
    for k in range(SHARED):
        top = jnp.max(keys)
        keys = jnp.where(keys == top, -1.0, keys)
        head = 31 - lax.rem(top.astype(jnp.int32), 32)
        used_ref[head] = 1
        slot_ref[2 * k + 1] = head
        slot_ref[2 * (k + SHARED) + 1] = head

    def place(h, filled):
        slot_ref[2 * filled] = h
        return filled + 1 - used_ref[h]

    lax.fori_loop(0, H, place, 0)
    copies = []
    for s in range(SLOTS):
        column = pl.multiple_of(slot_ref[s] * HD, HD)
        copy = pltpu.make_async_copy(x_ref.at[:, :, pl.ds(column, HD)], out_ref.at[s], sems.at[s])
        copy.start()
        copies.append(copy)
    for copy in copies:
        copy.wait()


def pack(counts, x):
    return pl.pallas_call(
        pack_kernel,
        out_shape=(
            jax.ShapeDtypeStruct((SLOTS, 3, x.shape[1], HD), x.dtype),
            jax.ShapeDtypeStruct((SLOTS + 8,), jnp.int32),
        ),
        in_specs=[pl.BlockSpec(memory_space=pltpu.VMEM), pl.BlockSpec(memory_space=pl.ANY)],
        out_specs=(pl.BlockSpec(memory_space=pl.ANY), pl.BlockSpec(memory_space=pltpu.SMEM)),
        scratch_shapes=[pltpu.SMEM((H,), jnp.int32), pltpu.SemaphoreType.DMA((SLOTS,))],
        cost_estimate=pl.CostEstimate(flops=0, bytes_accessed=25_000_000, transcendentals=0),
        name="pack_heads",
    )(counts, x)


def attend_kernel(
    slot_ref, class_ref, lists_ref, counts_ref, gate_ref, x_ref,
    first_ref, second_ref, rest_ref,
    held, result, sorted_ref, start_ref, in_sems, out_sems,
):
    pieces = in_sems.shape[0]
    width = x_ref.shape[0] // pieces
    loads = [
        pltpu.make_async_copy(
            x_ref.at[pl.ds(i * width, width)], held.at[pl.ds(i * width, width)], in_sems.at[i]
        )
        for i in range(pieces)
    ]
    for load in loads:
        load.start()

    me = lax.axis_index("seq")
    shared = lax.rem(me, 2)
    parity = me // (2 * SHARED)
    head = slot_ref[me]
    list_base = class_ref[head] * (TILE * KMAX)
    count_base = head * TILE
    ntiles = x_ref.shape[0] * 4

    for c in range(KMAX + 2):
        start_ref[c] = 0
    step = 1 + shared
    total = ntiles // step

    def tally(i, carry):
        count = counts_ref[count_base + i * step + shared * parity]
        start_ref[count + 1] = start_ref[count + 1] + 1
        return carry

    lax.fori_loop(0, total, tally, 0)
    begins = [jnp.int32(0)]
    for c in range(1, KMAX + 1):
        begins.append(begins[-1] + start_ref[c + 1])
    for c in range(1, KMAX + 1):
        start_ref[c] = begins[c - 1]

    def place(i, carry):
        tile = i * step + shared * parity
        count = counts_ref[count_base + tile]
        position = start_ref[count]
        sorted_ref[position] = tile
        start_ref[count] = position + 1
        return carry

    lax.fori_loop(0, total, place, 0)
    gate = gate_ref[:, pl.ds(pl.multiple_of(head * HD, HD), HD)].astype(jnp.float32)
    ones = jnp.ones((TILE, HD), jnp.bfloat16)
    for load in loads:
        load.wait()

    def tile_of(which, t):
        return held[t // 4, which, lax.rem(t, 4)]

    for c in range(1, KMAX + 1):
        group = max(1, PAIRS // c)
        begin, end = begins[c - 1], begins[c]

        def unit(i, carry, c=c, group=group, begin=begin, end=end):
            tiles = [
                sorted_ref[jnp.minimum(begin + i * group + u, end - 1)] for u in range(group)
            ]
            listed = [[lists_ref[list_base + t * KMAX + j] for j in range(c)] for t in tiles]
            scores = [
                lax.dot_general(
                    tile_of(0, t),
                    jnp.concatenate([tile_of(1, k) for k in keys], axis=0),
                    (((1,), (1,)), ((), ())),
                    preferred_element_type=jnp.float32,
                )
                for t, keys in zip(tiles, listed)
            ]
            raised = [
                jnp.exp2((s - jnp.max(s, axis=1, keepdims=True)) * (HD ** (-0.5) * LOG2E)).astype(
                    jnp.bfloat16
                )
                for s in scores
            ]
            mixed = [
                jnp.dot(
                    r,
                    jnp.concatenate(
                        [jnp.concatenate([tile_of(2, k), ones], axis=1) for k in keys], axis=0
                    ),
                    preferred_element_type=jnp.float32,
                )
                for r, keys in zip(raised, listed)
            ]
            for t, m in zip(tiles, mixed):
                attended = (m[:, :HD] / m[:, HD:]).astype(jnp.bfloat16)
                row = lax.rem(t, 4) - shared * parity
                result[row, t // 4] = (gate * attended.astype(jnp.float32)).astype(jnp.bfloat16)
            return carry

        lax.fori_loop(0, (end - begin + group - 1) // group, unit, 0)

    stores = [
        pltpu.make_async_copy(result.at[0], first_ref, out_sems.at[0]),
        pltpu.make_async_copy(result.at[1], second_ref, out_sems.at[1]),
        pltpu.make_async_copy(result.at[2], rest_ref.at[:, 0], out_sems.at[2]),
        pltpu.make_async_copy(result.at[3], rest_ref.at[:, 1], out_sems.at[3]),
    ]
    for store in stores:
        store.start()
    for store in stores:
        store.wait()


def attend(slots, head_class, lists, counts, gate, arrived):
    owners = arrived.shape[0]
    smem = pl.BlockSpec(memory_space=pltpu.SMEM)
    anywhere = pl.BlockSpec(memory_space=pl.ANY)
    part = jax.ShapeDtypeStruct((owners, TILE, HD), jnp.bfloat16)
    return pl.pallas_call(
        attend_kernel,
        out_shape=(part, part, jax.ShapeDtypeStruct((owners, 2, TILE, HD), jnp.bfloat16)),
        in_specs=[smem, smem, smem, smem, pl.BlockSpec(memory_space=pltpu.VMEM), anywhere],
        out_specs=(anywhere, anywhere, anywhere),
        scratch_shapes=[
            pltpu.VMEM(arrived.shape, jnp.bfloat16),
            pltpu.VMEM((4, owners, TILE, HD), jnp.bfloat16),
            pltpu.SMEM((owners * 4,), jnp.int32),
            pltpu.SMEM((KMAX + 2,), jnp.int32),
            pltpu.SemaphoreType.DMA((8,)),
            pltpu.SemaphoreType.DMA((4,)),
        ],
        compiler_params=pltpu.CompilerParams(vmem_limit_bytes=32 * 1024 * 1024),
        cost_estimate=pl.CostEstimate(
            flops=20_000_000_000, bytes_accessed=17_000_000, transcendentals=8_000_000
        ),
        name="attend_tiles",
    )(slots, head_class, lists, counts, gate, arrived)


def row_copies(slot_ref, rows_ref, out_ref, sems):
    copies = []
    for chip in range(CHIPS):
        column = pl.multiple_of(slot_ref[2 * chip] * HD, HD)
        for i in range(2):
            copies.append((rows_ref.at[2 * chip, i], i, column))
        column = pl.multiple_of(slot_ref[2 * chip + 1] * HD, HD)
        copies.append((rows_ref.at[2 * chip + 1, 0], chip // SHARED, column))
    return [
        pltpu.make_async_copy(
            source, out_ref.at[pl.ds(i * TILE, TILE), pl.ds(column, HD)], sems.at[n]
        )
        for n, (source, i, column) in enumerate(copies)
    ]


def unpack_kernel(slot_ref, rows_ref, out_ref, sems):
    copies = row_copies(slot_ref, rows_ref, out_ref, sems)
    for copy in copies:
        copy.start()
    for copy in copies:
        copy.wait()


def unpack(slots, rows):
    anywhere = pl.BlockSpec(memory_space=pl.ANY)
    return pl.pallas_call(
        unpack_kernel,
        out_shape=jax.ShapeDtypeStruct((2 * TILE, H * HD), rows.dtype),
        in_specs=[pl.BlockSpec(memory_space=pltpu.SMEM), anywhere],
        out_specs=anywhere,
        scratch_shapes=[pltpu.SemaphoreType.DMA((3 * CHIPS,))],
        cost_estimate=pl.CostEstimate(flops=0, bytes_accessed=3_000_000, transcendentals=0),
        name="unpack_rows",
    )(slots, rows)


def join_kernel(slot_ref, rows_ref, done_ref, out_ref, sems):
    half = 2 * TILE
    copies = row_copies(slot_ref, rows_ref, out_ref, sems)
    copies.append(
        pltpu.make_async_copy(done_ref, out_ref.at[pl.ds(half, half)], sems.at[len(copies)])
    )
    for copy in copies:
        copy.start()
    for copy in copies:
        copy.wait()


def join(slots, rows, done):
    anywhere = pl.BlockSpec(memory_space=pl.ANY)
    return pl.pallas_call(
        join_kernel,
        out_shape=jax.ShapeDtypeStruct((4 * TILE, H * HD), rows.dtype),
        in_specs=[pl.BlockSpec(memory_space=pltpu.SMEM), anywhere, anywhere],
        out_specs=anywhere,
        scratch_shapes=[pltpu.SemaphoreType.DMA((3 * CHIPS + 1,))],
        cost_estimate=pl.CostEstimate(flops=0, bytes_accessed=6_000_000, transcendentals=0),
        name="join_rows",
    )(slots, rows, done)


def next_section(block, senders):
    sections = lax.axis_size("section")
    owners = lax.axis_size("seq")
    route = [
        (z * owners + s, (z + 1) % sections * owners + s)
        for z in range(sections)
        for s in senders
    ]
    return lax.ppermute(block, ("section", "seq"), route)


def local(projected, gate, head_class, tile_lists, tile_counts):
    owners = lax.axis_size("seq")
    packed, slots = pack(tile_counts, projected[0])
    arrived = lax.all_to_all(packed, "seq", split_axis=0, concat_axis=0, tiled=True)
    arrived = arrived.reshape(owners, 3, 4, TILE, HD)
    first, second, rest = attend(
        slots, head_class, tile_lists.reshape(-1), tile_counts.reshape(-1), gate, arrived
    )
    first = next_section(first, range(owners))
    second = next_section(second, range(0, owners, 2))
    rest = lax.all_to_all(rest, "seq", split_axis=0, concat_axis=0, tiled=True)
    rest = next_section(unpack(slots, rest), range(owners))
    moved = lax.all_to_all(
        jnp.stack([first, second], axis=1), "seq", split_axis=0, concat_axis=0, tiled=True
    )
    return join(slots, moved, rest)[None]


def solution(mesh):
    placed = (P("section", None, "seq", None), P("section", None), P(), P(), P())
    return jax.shard_map(
        local, mesh=mesh, in_specs=placed, out_specs=P("section", "seq", None), check_vma=False
    )
```

time: 690 us -> 865 us (1.25)
  Pallas kernels: 0 us -> 563 us
  local copies, waits for them, and re-layouts: 174 us -> 0.27 us
  matrix products: 87.2 us -> 0 us
  blocking collectives: 81.7 us -> 0 us
  other arithmetic: 57.6 us -> 1.52 us
  starting transfers between devices: 10.5 us -> 59.5 us
  waiting for transfers between devices: 263 us -> 236 us
  loops' own time: 10.6 us -> 0 us
    pallas_call x0 -> x4, Pallas kernels: none -> 563 us  [the longest x1 384 us: pack(): pl.pallas_call(pack_kernel, out_shape=(jax.ShapeDtypeStruct((SLOTS, 3, x....]
    gather x32 -> x0, local copies, waits for them, and re-layouts: 100 us -> none  [the longest x16 50.2 us: one_group(): gathered_keys = key_tiles[group_rows].reshape(QG, kmax * tile_len, depth)]
    dot_general x32 -> x0, matrix products: 87.2 us -> none  [the longest x16 60.5 us: one_group(): jnp.einsum('qtk,qkd->qtd', weights, gathered_values, preferred_element_ty...]
    all_to_all x1 -> x0, blocking collectives: 81.7 us -> none  [local(): lax.all_to_all(shifted, 'seq', split_axis=1, concat_axis=1, tiled=True)]
    sub x16 -> x0, other arithmetic: 53.1 us -> none  [one_group(): raised = jnp.exp(scores - highest)]
    all_to_all x1 -> x3, starting transfers between devices: 8.77 us -> 57 us  [the longest x1 29.4 us: local(): rest = lax.all_to_all(rest, 'seq', split_axis=0, concat_axis=0, tiled=True)]
    ppermute x1 -> x3, waiting for transfers between devices: 91.2 us -> 62 us  [next_section(): return lax.ppermute(block, ('section', 'seq'), route)]
    transpose x2 -> x0, local copies, waits for them, and re-layouts: 26.2 us -> none  [local(): spread.reshape(3, local_len, slot_count, owners, HD)]
  transfers between devices with their start and end apart: 2 -> 6, of which waited for: 2 -> 3; matrix products, arithmetic and copies ran while one was open for 0% -> 0% of each run, Pallas kernels for 0% -> 6%
where the time goes in v1:
time: 865 us; the launch traced here: 861 us
  Pallas kernels  563 us (65%)
  waiting for transfers between devices  236 us (27%)
  starting transfers between devices  59.5 us (7%)
    pallas_call x1, Pallas kernels, pack(): pl.pallas_call(pack_kernel, out_shape=(jax.ShapeDtypeStruct((SLOTS, 3, x....  384 us
    all_to_all x1, waiting for transfers between devices, local(): lax.all_to_all(packed, 'seq', split_axis=0, concat_axis=0, tiled=True)  174 us
    pallas_call x1, Pallas kernels, join(): pl.pallas_call(join_kernel, out_shape=jax.ShapeDtypeStruct((4 * TILE, H *...  97.5 us
    ppermute x3, waiting for transfers between devices, next_section(): return lax.ppermute(block, ('section', 'seq'), route)  62 us
    pallas_call x1, Pallas kernels, unpack(): pl.pallas_call(unpack_kernel, out_shape=jax.ShapeDtypeStruct((2 * TILE, H...  49.9 us
    pallas_call x1, Pallas kernels, attend(): pl.pallas_call(attend_kernel, out_shape=(part, part, jax.ShapeDtypeStruct...  31.3 us
    all_to_all x1, starting transfers between devices, local(): rest = lax.all_to_all(rest, 'seq', split_axis=0, concat_axis=0, tiled=True)  29.4 us
    all_to_all x1, starting transfers between devices, local(): lax.all_to_all(jnp.stack([first, second], axis=1), 'seq', split_axis=0, c...  19 us
  transfers between devices with their start and end apart: 6, of which 3 were waited for; matrix products, arithmetic and copies ran while one was open for 0% of the time, Pallas kernels for 6%

profile of v1, /device:TPU:1, one launch (start us, length us, event | category | flops | bytes accessed | tf_op | source)
XLA Modules:
  0.0 861.0 jit_solution(8579735114332669782)
XLA Ops:
  0.0 384.4 %pack_heads.1 = (bf16[32,3,512,128]{3,2,1,0:T(8,128)(2,1)}, s32[40]{0:T(128)}) custom-call(s32[24,128]{1,0:T(8,128)} %counts_ref.1, bf16[3,512,3072]{2,1,0:T(8,128)(2,1)} %bitcast.7), custom_call_target="tpu_custom_call" | custom-call | bytes 25000000 | tf_op jit(solution)/shard_map/pack_heads/pallas_call | solution.py:53
  384.4 0.0 copy-start.5
  384.4 0.0 copy-start
  384.4 0.0 copy-start.2
  384.4 0.0 copy-start.3
  384.4 8.7 %all-to-all-start = ((bf16[32,3,512,128]{3,2,1,0:T(8,128)(2,1)}), bf16[32,3,512,128]{3,2,1,0:T(8,128)(2,1)}, u32[]{:S(2)}, u32[]{:S(2)}) async-start(bf16[32,3,512,128]{3,2,1,0:T(8,128)(2,1)} %get-tuple-element.11), calls=%async_computation | async-start | bytes 25165824 | tf_op jit(solution)/shard_map/all_to_all | solution.py:281
  393.1 0.1 copy.6
  393.2 0.1 reshape.9.lists_ref
  393.4 174.4 %all-to-all-done = bf16[32,3,512,128]{3,2,1,0:T(8,128)(2,1)} async-done(((bf16[32,3,512,128]{3,2,1,0:T(8,128)(2,1)}), bf16[32,3,512,128]{3,2,1,0:T(8,128)(2,1)}, u32[]{:S(2)}, u32[]{:S(2)}) %all-to-all-start) | async-done | bytes 12582944 | tf_op jit(solution)/shard_map/all_to_all | solution.py:281
  567.8 0.0 copy-done.2
  567.8 31.3 %attend_tiles.1 = (bf16[32,128,128]{2,1,0:T(8,128)(2,1)S(1)}, bf16[32,128,128]{2,1,0:T(8,128)(2,1)S(1)}, bf16[32,2,128,128]{3,2,1,0:T(8,128)(2,1)}) custom-call(s32[40]{0:T(128)S(1)} %copy-done.1, s32[24]{0:T(128)S(1)} %copy-done.3, s32[2048]{0:T(1024)S(1)} %reshape.9.lists_ref, s32[3072]{0:T(1024)S(1)} %bitcast.6, bf16[1,3072]{1,0:T(2,128)(2,1)S(1)} %copy-done.2, ...), custom_call_target="tpu_custom_call" | custom-call | flops 20000000000 | bytes 17000000 | tf_op jit(solution)/shard_map/attend_tiles/pallas_call | solution.py:184
  599.1 29.4 %all-to-all-start.2 = ((bf16[32,2,128,128]{3,2,1,0:T(8,128)(2,1)}), bf16[32,2,128,128]{3,2,1,0:T(8,128)(2,1)}, u32[]{:S(2)}, u32[]{:S(2)}) async-start(bf16[32,2,128,128]{3,2,1,0:T(8,128)(2,1)} %get-tuple-element.14), calls=%async_computation.2 | async-start | bytes 4194304 | tf_op jit(solution)/shard_map/all_to_all | solution.py:288
  628.5 1.7 collective-permute-start
  630.2 0.7 collective-permute-start.1
  630.9 24.8 %collective-permute-done = bf16[32,128,128]{2,1,0:T(8,128)(2,1)S(1)} collective-permute-done((bf16[32,128,128]{2,1,0:T(8,128)(2,1)S(1)}, bf16[32,128,128]{2,1,0:T(8,128)(2,1)S(1)}, u32[]{:S(2)}, u32[]{:S(2)}) %collective-permute-start) | collective-permute-done | bytes 1048608 | tf_op jit(solution)/shard_map/ppermute | solution.py:275
  655.7 0.0 collective-permute-done.1
  655.7 1.5 pad_maximum_fusion
  657.2 0.0 all-to-all-done.2.rows_ref
  657.2 19.0 %all-to-all-start.1 = ((bf16[32,2,128,128]{3,2,1,0:T(8,128)(2,1)}), bf16[32,2,128,128]{3,2,1,0:T(8,128)(2,1)S(1)}, u32[]{:S(2)}, u32[]{:S(2)}) async-start(bf16[32,2,128,128]{3,2,1,0:T(8,128)(2,1)} %pad_maximum_fusion), calls=%async_computation.1 | async-start | bytes 4194304 | tf_op jit(solution)/shard_map/all_to_all | solution.py:290
  676.2 49.9 %unpack_rows.1 = bf16[256,3072]{1,0:T(8,128)(2,1)} custom-call(s32[40]{0:T(128)} %get-tuple-element.10.slot_ref, bf16[32,2,128,128]{3,2,1,0:T(8,128)(2,1)} %all-to-all-done.2.rows_ref), custom_call_target="tpu_custom_call" | custom-call | bytes 3000000 | tf_op jit(solution)/shard_map/unpack_rows/pallas_call | solution.py:231
  726.1 0.1 collective-permute-start.2
  726.2 0.0 all-to-all-done.1.rows_ref
  726.2 37.3 %collective-permute-done.2.done_ref = bf16[256,3072]{1,0:T(8,128)(2,1)} collective-permute-done((bf16[256,3072]{1,0:T(8,128)(2,1)}, bf16[256,3072]{1,0:T(8,128)(2,1)}, u32[]{:S(2)}, u32[]{:S(2)}) %collective-permute-start.2) | collective-permute-done | bytes 1572896 | tf_op jit(solution)/shard_map/ppermute | solution.py:275
  763.4 97.5 %join_rows.1 = bf16[512,3072]{1,0:T(8,128)(2,1)} custom-call(s32[40]{0:T(128)} %get-tuple-element.10.slot_ref, bf16[32,2,128,128]{3,2,1,0:T(8,128)(2,1)} %copy-done.4, bf16[256,3072]{1,0:T(8,128)(2,1)} %collective-permute-done.2.done_ref), custom_call_target="tpu_custom_call" | custom-call | bytes 6000000 | tf_op jit(solution)/shard_map/join_rows/pallas_call | solution.py:256
  (7 shorter events, 0.0 us)
Async XLA Ops:
  384.4 8.7 %copy-start.5 = (s32[2,128,8]{1,2,0:T(8,128)S(1)}, s32[2,128,8]{1,2,0:T(8,128)}, u32[]{:S(2)}) copy-start(s32[2,128,8]{1,2,0:T(8,128)} %param.8) | copy-start | bytes 24580
  384.4 183.4 %copy-start = (s32[24,128]{1,0:T(8,128)S(1)}, s32[24,128]{1,0:T(8,128)}, u32[]{:S(2)}) copy-start(s32[24,128]{1,0:T(8,128)} %counts_ref.1) | copy-start | bytes 36868
  384.4 183.4 %copy-start.1 = (s32[40]{0:T(128)S(1)}, s32[40]{0:T(128)}, u32[]{:S(2)}) copy-start(s32[40]{0:T(128)} %get-tuple-element.10.slot_ref) | copy-start | bytes 484
  384.4 183.3 %copy-start.2 = (bf16[1,3072]{1,0:T(2,128)(2,1)S(1)}, bf16[1,3072]{1,0:T(2,128)(2,1)}, u32[]{:S(2)}) copy-start(bf16[1,3072]{1,0:T(2,128)(2,1)} %gate_ref.1) | copy-start | bytes 18436
  384.4 183.3 %copy-start.3 = (s32[24]{0:T(128)S(1)}, s32[24]{0:T(128)}, u32[]{:S(2)}) copy-start(s32[24]{0:T(128)} %class_ref.1) | copy-start | bytes 292
  384.4 183.3 %all-to-all-start = ((bf16[32,3,512,128]{3,2,1,0:T(8,128)(2,1)}), bf16[32,3,512,128]{3,2,1,0:T(8,128)(2,1)}, u32[]{:S(2)}, u32[]{:S(2)}) async-start(bf16[32,3,512,128]{3,2,1,0:T(8,128)(2,1)} %get-tuple-element.11), calls=%async_computation | async-start | bytes 25165824 | tf_op jit(solution)/shard_map/all_to_all | solution.py:281
  599.1 58.1 %all-to-all-start.2 = ((bf16[32,2,128,128]{3,2,1,0:T(8,128)(2,1)}), bf16[32,2,128,128]{3,2,1,0:T(8,128)(2,1)}, u32[]{:S(2)}, u32[]{:S(2)}) async-start(bf16[32,2,128,128]{3,2,1,0:T(8,128)(2,1)} %get-tuple-element.14), calls=%async_computation.2 | async-start | bytes 4194304 | tf_op jit(solution)/shard_map/all_to_all | solution.py:288
  628.5 27.2 %collective-permute-start = (bf16[32,128,128]{2,1,0:T(8,128)(2,1)S(1)}, bf16[32,128,128]{2,1,0:T(8,128)(2,1)S(1)}, u32[]{:S(2)}, u32[]{:S(2)}) collective-permute-start(bf16[32,128,128]{2,1,0:T(8,128)(2,1)S(1)} %get-tuple-element.12), channel_id=1, source_target_pairs={{0,32},{1,33},{2,34},{3,35},{4,36},{5,37},{6,38},{7,39},{8,40},{9,... | collective-permute-start | bytes 3145736 | tf_op jit(solution)/shard_map/ppermute | solution.py:275
  630.2 25.5 %collective-permute-start.1 = (bf16[32,128,128]{2,1,0:T(8,128)(2,1)S(1)}, bf16[32,128,128]{2,1,0:T(8,128)(2,1)S(1)}, u32[]{:S(2)}, u32[]{:S(2)}) collective-permute-start(bf16[32,128,128]{2,1,0:T(8,128)(2,1)S(1)} %get-tuple-element.13), channel_id=1, source_target_pairs={{0,32},{2,34},{4,36},{6,38},{8,40},{10,42},{12,44},{14,46},{16,48}... | collective-permute-start | bytes 3145736 | tf_op jit(solution)/shard_map/ppermute | solution.py:275
  657.2 69.0 %all-to-all-start.1 = ((bf16[32,2,128,128]{3,2,1,0:T(8,128)(2,1)}), bf16[32,2,128,128]{3,2,1,0:T(8,128)(2,1)S(1)}, u32[]{:S(2)}, u32[]{:S(2)}) async-start(bf16[32,2,128,128]{3,2,1,0:T(8,128)(2,1)} %pad_maximum_fusion), calls=%async_computation.1 | async-start | bytes 4194304 | tf_op jit(solution)/shard_map/all_to_all | solution.py:290
  726.1 37.4 %collective-permute-start.2 = (bf16[256,3072]{1,0:T(8,128)(2,1)}, bf16[256,3072]{1,0:T(8,128)(2,1)}, u32[]{:S(2)}, u32[]{:S(2)}) collective-permute-start(bf16[256,3072]{1,0:T(8,128)(2,1)} %unpack_rows.1), channel_id=1, source_target_pairs={{0,32},{1,33},{2,34},{3,35},{4,36},{5,37},{6,38},{7,39},{8,40},{9,... | collective-permute-start | bytes 4718600 | tf_op jit(solution)/shard_map/ppermute | solution.py:275
  726.2 37.3 %copy-start.4 = (bf16[32,2,128,128]{3,2,1,0:T(8,128)(2,1)}, bf16[32,2,128,128]{3,2,1,0:T(8,128)(2,1)S(1)}, u32[]{:S(2)}) copy-start(bf16[32,2,128,128]{3,2,1,0:T(8,128)(2,1)S(1)} %all-to-all-done.1.rows_ref) | copy-start | bytes 6291460

commit v2 on v1

--- a/solution.py
+++ b/solution.py
@@ -16,7 +16,13 @@
 LOG2E = 1.4426950408889634
 
 
-def pack_kernel(counts_ref, x_ref, out_ref, slot_ref, used_ref, sems):
+def pack_kernel(counts_ref, x_ref, out_ref, slot_ref, held, used_ref, in_sems, sems):
+    rows = x_ref.shape[1] // 2
+    arrivals = []
+    for n in range(6):
+        part = (n // 2, pl.ds(n % 2 * rows, rows))
+        arrivals.append(pltpu.make_async_copy(x_ref.at[part], held.at[part], in_sems.at[n]))
+        arrivals[-1].start()
     loads = jnp.sum(counts_ref[...].astype(jnp.float32), axis=1, keepdims=True)
     order = lax.broadcasted_iota(jnp.int32, (H, 1), 0).astype(jnp.float32)
     keys = loads * 32.0 + (31.0 - order)
@@ -39,10 +45,12 @@
         return filled + 1 - used_ref[h]
 
     lax.fori_loop(0, H, place, 0)
+    for arrival in arrivals:
+        arrival.wait()
     copies = []
     for s in range(SLOTS):
         column = pl.multiple_of(slot_ref[s] * HD, HD)
-        copy = pltpu.make_async_copy(x_ref.at[:, :, pl.ds(column, HD)], out_ref.at[s], sems.at[s])
+        copy = pltpu.make_async_copy(held.at[:, :, pl.ds(column, HD)], out_ref.at[s], sems.at[s])
         copy.start()
         copies.append(copy)
     for copy in copies:
@@ -58,7 +66,13 @@
         ),
         in_specs=[pl.BlockSpec(memory_space=pltpu.VMEM), pl.BlockSpec(memory_space=pl.ANY)],
         out_specs=(pl.BlockSpec(memory_space=pl.ANY), pl.BlockSpec(memory_space=pltpu.SMEM)),
-        scratch_shapes=[pltpu.SMEM((H,), jnp.int32), pltpu.SemaphoreType.DMA((SLOTS,))],
+        scratch_shapes=[
+            pltpu.VMEM(x.shape, x.dtype),
+            pltpu.SMEM((H,), jnp.int32),
+            pltpu.SemaphoreType.DMA((6,)),
+            pltpu.SemaphoreType.DMA((SLOTS,)),
+        ],
+        compiler_params=pltpu.CompilerParams(vmem_limit_bytes=32 * 1024 * 1024),
         cost_estimate=pl.CostEstimate(flops=0, bytes_accessed=25_000_000, transcendentals=0),
         name="pack_heads",
     )(counts, x)
@@ -84,8 +98,7 @@
     shared = lax.rem(me, 2)
     parity = me // (2 * SHARED)
     head = slot_ref[me]
-    list_base = class_ref[head] * (TILE * KMAX)
-    count_base = head * TILE
+    list_base = class_ref[head] * KMAX
     ntiles = x_ref.shape[0] * 4
 
     for c in range(KMAX + 2):
@@ -94,7 +107,7 @@
     total = ntiles // step
 
     def tally(i, carry):
-        count = counts_ref[count_base + i * step + shared * parity]
+        count = counts_ref[head, i * step + shared * parity]
         start_ref[count + 1] = start_ref[count + 1] + 1
         return carry
 
@@ -107,7 +120,7 @@
 
     def place(i, carry):
         tile = i * step + shared * parity
-        count = counts_ref[count_base + tile]
+        count = counts_ref[head, tile]
         position = start_ref[count]
         sorted_ref[position] = tile
         start_ref[count] = position + 1
@@ -130,7 +143,7 @@
             tiles = [
                 sorted_ref[jnp.minimum(begin + i * group + u, end - 1)] for u in range(group)
             ]
-            listed = [[lists_ref[list_base + t * KMAX + j] for j in range(c)] for t in tiles]
+            listed = [[lists_ref[list_base + j, t] for j in range(c)] for t in tiles]
             scores = [
                 lax.dot_general(
                     tile_of(0, t),
@@ -202,66 +215,44 @@
     )(slots, head_class, lists, counts, gate, arrived)
 
 
-def row_copies(slot_ref, rows_ref, out_ref, sems):
-    copies = []
-    for chip in range(CHIPS):
-        column = pl.multiple_of(slot_ref[2 * chip] * HD, HD)
+def place_rows(slot_ref, rows_ref, out_ref):
+    def one_chip(chip, carry):
+        columns = pl.ds(pl.multiple_of(slot_ref[2 * chip] * HD, HD), HD)
         for i in range(2):
-            copies.append((rows_ref.at[2 * chip, i], i, column))
-        column = pl.multiple_of(slot_ref[2 * chip + 1] * HD, HD)
-        copies.append((rows_ref.at[2 * chip + 1, 0], chip // SHARED, column))
-    return [
-        pltpu.make_async_copy(
-            source, out_ref.at[pl.ds(i * TILE, TILE), pl.ds(column, HD)], sems.at[n]
-        )
-        for n, (source, i, column) in enumerate(copies)
-    ]
-
-
-def unpack_kernel(slot_ref, rows_ref, out_ref, sems):
-    copies = row_copies(slot_ref, rows_ref, out_ref, sems)
-    for copy in copies:
-        copy.start()
-    for copy in copies:
-        copy.wait()
-
-
-def unpack(slots, rows):
-    anywhere = pl.BlockSpec(memory_space=pl.ANY)
+            out_ref[i * TILE : (i + 1) * TILE, columns] = rows_ref[2 * chip, i]
+        columns = pl.ds(pl.multiple_of(slot_ref[2 * chip + 1] * HD, HD), HD)
+        start = pl.multiple_of(chip // SHARED * TILE, TILE)
+        out_ref[pl.ds(start, TILE), columns] = rows_ref[2 * chip + 1, 0]
+        return carry
+
+    lax.fori_loop(0, CHIPS, one_chip, 0)
+
+
+def join_kernel(slot_ref, rows_ref, done_ref, out_ref):
+    place_rows(slot_ref, rows_ref, out_ref)
+    half = done_ref.shape[0]
+    out_ref[half:, :] = done_ref[...]
+
+
+def stack_kernel(first_ref, second_ref, after_ref, out_ref):
+    out_ref[:, 0] = first_ref[...]
+    out_ref[:, 1] = second_ref[...]
+
+
+def copy_kernel(in_ref, out_ref):
+    out_ref[...] = in_ref[...]
+
+
+def on_vmem(body, shape, kinds, name, moved):
     return pl.pallas_call(
-        unpack_kernel,
-        out_shape=jax.ShapeDtypeStruct((2 * TILE, H * HD), rows.dtype),
-        in_specs=[pl.BlockSpec(memory_space=pltpu.SMEM), anywhere],
-        out_specs=anywhere,
-        scratch_shapes=[pltpu.SemaphoreType.DMA((3 * CHIPS,))],
-        cost_estimate=pl.CostEstimate(flops=0, bytes_accessed=3_000_000, transcendentals=0),
-        name="unpack_rows",
-    )(slots, rows)
-
-
-def join_kernel(slot_ref, rows_ref, done_ref, out_ref, sems):
-    half = 2 * TILE
-    copies = row_copies(slot_ref, rows_ref, out_ref, sems)
-    copies.append(
-        pltpu.make_async_copy(done_ref, out_ref.at[pl.ds(half, half)], sems.at[len(copies)])
+        body,
+        out_shape=jax.ShapeDtypeStruct(shape, jnp.bfloat16),
+        in_specs=[pl.BlockSpec(memory_space=kind) for kind in kinds],
+        out_specs=pl.BlockSpec(memory_space=pltpu.VMEM),
+        compiler_params=pltpu.CompilerParams(vmem_limit_bytes=32 * 1024 * 1024),
+        cost_estimate=pl.CostEstimate(flops=0, bytes_accessed=moved, transcendentals=0),
+        name=name,
     )
-    for copy in copies:
-        copy.start()
-    for copy in copies:
-        copy.wait()
-
-
-def join(slots, rows, done):
-    anywhere = pl.BlockSpec(memory_space=pl.ANY)
-    return pl.pallas_call(
-        join_kernel,
-        out_shape=jax.ShapeDtypeStruct((4 * TILE, H * HD), rows.dtype),
-        in_specs=[pl.BlockSpec(memory_space=pltpu.SMEM), anywhere, anywhere],
-        out_specs=anywhere,
-        scratch_shapes=[pltpu.SemaphoreType.DMA((3 * CHIPS + 1,))],
-        cost_estimate=pl.CostEstimate(flops=0, bytes_accessed=6_000_000, transcendentals=0),
-        name="join_rows",
-    )(slots, rows, done)
 
 
 def next_section(block, senders):
@@ -280,17 +271,24 @@
     packed, slots = pack(tile_counts, projected[0])
     arrived = lax.all_to_all(packed, "seq", split_axis=0, concat_axis=0, tiled=True)
     arrived = arrived.reshape(owners, 3, 4, TILE, HD)
-    first, second, rest = attend(
-        slots, head_class, tile_lists.reshape(-1), tile_counts.reshape(-1), gate, arrived
-    )
+    lists = tile_lists.transpose(0, 2, 1).reshape(-1, tile_lists.shape[1])
+    first, second, rest = attend(slots, head_class, lists, tile_counts, gate, arrived)
     first = next_section(first, range(owners))
     second = next_section(second, range(0, owners, 2))
+    smem, vmem = pltpu.SMEM, pltpu.VMEM
+    rest = on_vmem(copy_kernel, rest.shape, [vmem], "ready_rows", 4_000_000)(rest)
     rest = lax.all_to_all(rest, "seq", split_axis=0, concat_axis=0, tiled=True)
-    rest = next_section(unpack(slots, rest), range(owners))
-    moved = lax.all_to_all(
-        jnp.stack([first, second], axis=1), "seq", split_axis=0, concat_axis=0, tiled=True
+    half = (2 * TILE, H * HD)
+    done = on_vmem(place_rows, half, [smem, vmem], "place_rows", 4_000_000)(slots, rest)
+    done = next_section(done, range(owners))
+    stacked = on_vmem(stack_kernel, rest.shape, [vmem, vmem, pl.ANY], "stack_rows", 4_000_000)(
+        first, second, rest
     )
-    return join(slots, moved, rest)[None]
+    moved = lax.all_to_all(stacked, "seq", split_axis=0, concat_axis=0, tiled=True)
+    whole = (2 * half[0], half[1])
+    return on_vmem(join_kernel, whole, [smem, vmem, vmem], "join_rows", 6_000_000)(
+        slots, moved, done
+    )[None]
 
 
 def solution(mesh):

time: 865 us -> 303 us (0.35)
  Pallas kernels: 563 us -> 39.9 us
  waiting for transfers between devices: 236 us -> 61.9 us
  blocking collectives: 0 us -> 149 us
  starting transfers between devices: 59.5 us -> 34.3 us
  local copies, waits for them, and re-layouts: 0.27 us -> 15.7 us
    pallas_call x1, Pallas kernels: 384 us -> 5.69 us  [pack(): pl.pallas_call(pack_kernel, out_shape=(jax.ShapeDtypeStruct((SLOTS, 3, x....]
    all_to_all x2 -> x1, waiting for transfers between devices: 174 us -> 0.01 us  [local(): lax.all_to_all(stacked, 'seq', split_axis=0, concat_axis=0, tiled=True)]
    all_to_all x0 -> x1, blocking collectives: none -> 149 us  [local(): lax.all_to_all(packed, 'seq', split_axis=0, concat_axis=0, tiled=True)]
    pallas_call x2 -> x4, Pallas kernels: 147 us -> 5.1 us  [the longest x1 3.83 us: local(): on_vmem(join_kernel, whole, [smem, vmem, vmem], 'join_rows', 6000000)]
    all_to_all x1, starting transfers between devices: 29.4 us -> 12.8 us  [local(): rest = lax.all_to_all(rest, 'seq', split_axis=0, concat_axis=0, tiled=True)]
    unnamed x13 -> x24, local copies, waits for them, and re-layouts: 0.16 us -> 15.7 us
    all_to_all x2 -> x1, starting transfers between devices: 27.6 us -> 19 us  [local(): lax.all_to_all(stacked, 'seq', split_axis=0, concat_axis=0, tiled=True)]
  transfers between devices with their start and end apart: 6 -> 5, of which waited for: 3 -> 2; matrix products, arithmetic and copies ran while one was open for 0% -> 0% of each run, Pallas kernels for 6% -> 0%
where the time goes in v2:
time: 303 us; the launch traced here: 301 us
  blocking collectives  149 us (49%)
  waiting for transfers between devices  61.9 us (20%)
  Pallas kernels  39.9 us (13%)
  starting transfers between devices  34.3 us (11%)
  local copies, waits for them, and re-layouts  15.7 us (5%)
    all_to_all x1, blocking collectives, local(): lax.all_to_all(packed, 'seq', split_axis=0, concat_axis=0, tiled=True)  149 us
    ppermute x3, waiting for transfers between devices, next_section(): return lax.ppermute(block, ('section', 'seq'), route)  61.9 us
    pallas_call x1, Pallas kernels, attend(): pl.pallas_call(attend_kernel, out_shape=(part, part, jax.ShapeDtypeStruct...  29.1 us
    all_to_all x1, starting transfers between devices, local(): lax.all_to_all(stacked, 'seq', split_axis=0, concat_axis=0, tiled=True)  19 us
    unnamed x24, local copies, waits for them, and re-layouts  15.7 us
    all_to_all x1, starting transfers between devices, local(): rest = lax.all_to_all(rest, 'seq', split_axis=0, concat_axis=0, tiled=True)  12.8 us
  transfers between devices with their start and end apart: 5, of which 2 were waited for; matrix products, arithmetic and copies ran while one was open for 0% of the time, Pallas kernels for 0%

profile of v2, /device:TPU:1, one launch (start us, length us, event | category | flops | bytes accessed | tf_op | source)
XLA Modules:
  0.0 301.2 jit_solution(2161909907698864395)
XLA Ops:
  0.0 3.7 %copy-done.1 = bf16[1,3,512,3072]{3,2,1,0:T(8,128)(2,1)S(1)} copy-done((bf16[1,3,512,3072]{3,2,1,0:T(8,128)(2,1)S(1)}, bf16[1,3,512,3072]{3,2,1,0:T(8,128)(2,1)}, u32[]{:S(2)}) %copy-start.1) | copy-done | bytes 9437208
  3.7 0.7 copy-done.6
  4.4 5.7 %pack_heads.1 = (bf16[32,3,512,128]{3,2,1,0:T(8,128)(2,1)S(1)}, s32[40]{0:T(128)S(1)}) custom-call(s32[24,128]{1,0:T(8,128)S(1)} %copy-done.6, bf16[3,512,3072]{2,1,0:T(8,128)(2,1)S(1)} %bitcast.7), custom_call_target="tpu_custom_call" | custom-call | bytes 25000000 | tf_op jit(solution)/shard_map/pack_heads/pallas_call | solution.py:61
  10.1 4.5 %copy-done = bf16[32,3,512,128]{3,2,1,0:T(8,128)(2,1)} copy-done((bf16[32,3,512,128]{3,2,1,0:T(8,128)(2,1)}, bf16[32,3,512,128]{3,2,1,0:T(8,128)(2,1)S(1)}, u32[]{:S(2)}) %copy-start) | copy-done | bytes 12582936
  14.6 149.2 %all_to_all.15 = bf16[32,3,512,128]{3,2,1,0:T(8,128)(2,1)S(1)} all-to-all(bf16[32,3,512,128]{3,2,1,0:T(8,128)(2,1)} %copy-done), channel_id=1, replica_groups=mesh['section'=4,'seq'=32] {'seq'}, dimensions={0} | all-to-all | bytes 25165824 | tf_op jit(solution)/shard_map/all_to_all | solution.py:272
  163.9 29.1 %attend_tiles.1 = (bf16[32,128,128]{2,1,0:T(8,128)(2,1)S(1)}, bf16[32,128,128]{2,1,0:T(8,128)(2,1)S(1)}, bf16[32,2,128,128]{3,2,1,0:T(8,128)(2,1)S(1)}) custom-call(s32[40]{0:T(128)S(1)} %get-tuple-element.10.slot_ref, s32[24]{0:T(128)S(1)} %copy-done.11, s32[16,128]{1,0:T(8,128)S(1)} %bitcast.8, s32[24,128]{1,0:T(8,128)S(1)} %copy-done.6, ...), custom_call_target="tpu_custom_call" | custom-call | flops 20000000000 | bytes 17000000 | tf_op jit(solution)/shard_map/attend_tiles/pallas_call | solution.py:197
  193.0 1.0 copy-done.7
  194.0 1.0 copy-done.8
  195.0 0.1 ready_rows.1
  195.1 0.0 copy-start.3
  195.1 1.3 copy-done.3
  196.4 12.8 %all-to-all-start.1 = ((bf16[32,2,128,128]{3,2,1,0:T(8,128)(2,1)}), bf16[32,2,128,128]{3,2,1,0:T(8,128)(2,1)S(1)}, u32[]{:S(2)}, u32[]{:S(2)}) async-start(bf16[32,2,128,128]{3,2,1,0:T(8,128)(2,1)} %copy-done.3), calls=%async_computation.1 | async-start | bytes 4194304 | tf_op jit(solution)/shard_map/all_to_all | solution.py:280
  209.2 1.7 collective-permute-start
  210.9 0.7 collective-permute-start.1
  211.7 25.0 %collective-permute-done.first_ref = bf16[32,128,128]{2,1,0:T(8,128)(2,1)S(1)} collective-permute-done((bf16[32,128,128]{2,1,0:T(8,128)(2,1)}, bf16[32,128,128]{2,1,0:T(8,128)(2,1)S(1)}, u32[]{:S(2)}, u32[]{:S(2)}) %collective-permute-start) | collective-permute-done | bytes 1048608 | tf_op jit(solution)/shard_map/ppermute | solution.py:266
  236.7 1.0 copy-done.4
  237.7 1.2 copy-done.5
  238.9 0.1 stack_rows.1
  239.0 1.3 copy-done.2
  240.3 19.0 %all-to-all-start.2 = ((bf16[32,2,128,128]{3,2,1,0:T(8,128)(2,1)}), bf16[32,2,128,128]{3,2,1,0:T(8,128)(2,1)}, u32[]{:S(2)}, u32[]{:S(2)}) async-start(bf16[32,2,128,128]{3,2,1,0:T(8,128)(2,1)} %copy-done.2), calls=%async_computation.2 | async-start | bytes 4194304 | tf_op jit(solution)/shard_map/all_to_all | solution.py:287
  259.4 1.0 place_rows.1
  260.4 0.1 collective-permute-start.2
  260.5 36.9 %collective-permute-done.2.done_ref = bf16[256,3072]{1,0:T(8,128)(2,1)S(1)} collective-permute-done((bf16[256,3072]{1,0:T(8,128)(2,1)S(1)}, bf16[256,3072]{1,0:T(8,128)(2,1)S(1)}, u32[]{:S(2)}, u32[]{:S(2)}) %collective-permute-start.2) | collective-permute-done | bytes 1572896 | tf_op jit(solution)/shard_map/ppermute | solution.py:266
  297.4 3.8 %join_rows.1 = bf16[512,3072]{1,0:T(8,128)(2,1)} custom-call(s32[40]{0:T(128)S(1)} %get-tuple-element.10.slot_ref, bf16[32,2,128,128]{3,2,1,0:T(8,128)(2,1)} %all-to-all-done.2.rows_ref, bf16[256,3072]{1,0:T(8,128)(2,1)S(1)} %collective-permute-done.2.done_ref), custom_call_target="tpu_custom_call" | custom-call | bytes 6000000 | tf_op jit(solution)/shard_map/join_rows/pallas_call | solution.py:289
  (17 shorter events, 0.0 us)
Async XLA Ops:
  0.0 3.7 %copy-start.1 = (bf16[1,3,512,3072]{3,2,1,0:T(8,128)(2,1)S(1)}, bf16[1,3,512,3072]{3,2,1,0:T(8,128)(2,1)}, u32[]{:S(2)}) copy-start(bf16[1,3,512,3072]{3,2,1,0:T(8,128)(2,1)} %param.5) | copy-start | bytes 28311556
  3.7 0.7 copy-start.6
  10.1 4.5 %copy-start = (bf16[32,3,512,128]{3,2,1,0:T(8,128)(2,1)}, bf16[32,3,512,128]{3,2,1,0:T(8,128)(2,1)S(1)}, u32[]{:S(2)}) copy-start(bf16[32,3,512,128]{3,2,1,0:T(8,128)(2,1)S(1)} %get-tuple-element.11) | copy-start | bytes 37748740
  14.6 149.2 %copy-start.9 = (bf16[1,3072]{1,0:T(2,128)(2,1)S(1)}, bf16[1,3072]{1,0:T(2,128)(2,1)}, u32[]{:S(2)}) copy-start(bf16[1,3072]{1,0:T(2,128)(2,1)} %gate_ref.1) | copy-start | bytes 18436
  14.6 149.2 %copy-start.10 = (s32[2,128,8]{1,2,0:T(8,128)S(1)}, s32[2,128,8]{1,2,0:T(8,128)}, u32[]{:S(2)}) copy-start(s32[2,128,8]{1,2,0:T(8,128)} %param.8) | copy-start | bytes 24580
  14.6 149.2 %copy-start.11 = (s32[24]{0:T(128)S(1)}, s32[24]{0:T(128)}, u32[]{:S(2)}) copy-start(s32[24]{0:T(128)} %class_ref.1) | copy-start | bytes 292
  193.0 1.0 copy-start.7
  194.0 1.0 copy-start.8
  195.1 1.3 copy-start.3
  196.4 41.2 %all-to-all-start.1 = ((bf16[32,2,128,128]{3,2,1,0:T(8,128)(2,1)}), bf16[32,2,128,128]{3,2,1,0:T(8,128)(2,1)S(1)}, u32[]{:S(2)}, u32[]{:S(2)}) async-start(bf16[32,2,128,128]{3,2,1,0:T(8,128)(2,1)} %copy-done.3), calls=%async_computation.1 | async-start | bytes 4194304 | tf_op jit(solution)/shard_map/all_to_all | solution.py:280
  209.2 27.4 %collective-permute-start = (bf16[32,128,128]{2,1,0:T(8,128)(2,1)}, bf16[32,128,128]{2,1,0:T(8,128)(2,1)S(1)}, u32[]{:S(2)}, u32[]{:S(2)}) collective-permute-start(bf16[32,128,128]{2,1,0:T(8,128)(2,1)} %copy-done.8), channel_id=1, source_target_pairs={{0,32},{1,33},{2,34},{3,35},{4,36},{5,37},{6,38},{7,39},{8,40},{9,... | collective-permute-start | bytes 3145736 | tf_op jit(solution)/shard_map/ppermute | solution.py:266
  210.9 25.7 %collective-permute-start.1 = (bf16[32,128,128]{2,1,0:T(8,128)(2,1)}, bf16[32,128,128]{2,1,0:T(8,128)(2,1)S(1)}, u32[]{:S(2)}, u32[]{:S(2)}) collective-permute-start(bf16[32,128,128]{2,1,0:T(8,128)(2,1)} %copy-done.7), channel_id=1, source_target_pairs={{0,32},{2,34},{4,36},{6,38},{8,40},{10,42},{12,44},{14,46},{16,48}... | collective-permute-start | bytes 3145736 | tf_op jit(solution)/shard_map/ppermute | solution.py:266
  236.7 1.0 copy-start.4
  237.7 1.2 copy-start.5
  239.0 1.3 copy-start.2
  240.3 57.0 %all-to-all-start.2 = ((bf16[32,2,128,128]{3,2,1,0:T(8,128)(2,1)}), bf16[32,2,128,128]{3,2,1,0:T(8,128)(2,1)}, u32[]{:S(2)}, u32[]{:S(2)}) async-start(bf16[32,2,128,128]{3,2,1,0:T(8,128)(2,1)} %copy-done.2), calls=%async_computation.2 | async-start | bytes 4194304 | tf_op jit(solution)/shard_map/all_to_all | solution.py:287
  260.4 37.0 %collective-permute-start.2 = (bf16[256,3072]{1,0:T(8,128)(2,1)S(1)}, bf16[256,3072]{1,0:T(8,128)(2,1)S(1)}, u32[]{:S(2)}, u32[]{:S(2)}) collective-permute-start(bf16[256,3072]{1,0:T(8,128)(2,1)S(1)} %place_rows.1), channel_id=1, source_target_pairs={{0,32},{1,33},{2,34},{3,35},{4,36},{5,37},{6,38},{7,39},{8,40},{9,... | collective-permute-start | bytes 4718600 | tf_op jit(solution)/shard_map/ppermute | solution.py:266

commit v3 on v2

--- a/solution.py
+++ b/solution.py
@@ -10,7 +10,7 @@
 TILE = 128
 KMAX = 8
 SHARED = 8
-PAIRS = 8
+PAIRS = 32
 CHIPS = 16
 SLOTS = 2 * CHIPS
 LOG2E = 1.4426950408889634
@@ -45,14 +45,17 @@
         return filled + 1 - used_ref[h]
 
     lax.fori_loop(0, H, place, 0)
-    for arrival in arrivals:
-        arrival.wait()
     copies = []
-    for s in range(SLOTS):
-        column = pl.multiple_of(slot_ref[s] * HD, HD)
-        copy = pltpu.make_async_copy(held.at[:, :, pl.ds(column, HD)], out_ref.at[s], sems.at[s])
-        copy.start()
-        copies.append(copy)
+    for which in range(3):
+        arrivals[2 * which].wait()
+        arrivals[2 * which + 1].wait()
+        for s in range(SLOTS):
+            columns = pl.ds(pl.multiple_of(slot_ref[s] * HD, HD), HD)
+            copy = pltpu.make_async_copy(
+                held.at[which, :, columns], out_ref.at[s, which], sems.at[which, s]
+            )
+            copy.start()
+            copies.append(copy)
     for copy in copies:
         copy.wait()
 
@@ -70,9 +73,9 @@
             pltpu.VMEM(x.shape, x.dtype),
             pltpu.SMEM((H,), jnp.int32),
             pltpu.SemaphoreType.DMA((6,)),
-            pltpu.SemaphoreType.DMA((SLOTS,)),
+            pltpu.SemaphoreType.DMA((3, SLOTS)),
         ],
-        compiler_params=pltpu.CompilerParams(vmem_limit_bytes=32 * 1024 * 1024),
+        compiler_params=pltpu.CompilerParams(vmem_limit_bytes=60 * 1024 * 1024),
         cost_estimate=pl.CostEstimate(flops=0, bytes_accessed=25_000_000, transcendentals=0),
         name="pack_heads",
     )(counts, x)
@@ -111,7 +114,7 @@
         start_ref[count + 1] = start_ref[count + 1] + 1
         return carry
 
-    lax.fori_loop(0, total, tally, 0)
+    lax.fori_loop(0, total // 8, lambda i, carry: [tally(8 * i + u, 0) for u in range(8)][-1], 0)
     begins = [jnp.int32(0)]
     for c in range(1, KMAX + 1):
         begins.append(begins[-1] + start_ref[c + 1])
@@ -126,7 +129,7 @@
         start_ref[count] = position + 1
         return carry
 
-    lax.fori_loop(0, total, place, 0)
+    lax.fori_loop(0, total // 8, lambda i, carry: [place(8 * i + u, 0) for u in range(8)][-1], 0)
     gate = gate_ref[:, pl.ds(pl.multiple_of(head * HD, HD), HD)].astype(jnp.float32)
     ones = jnp.ones((TILE, HD), jnp.bfloat16)
     for load in loads:
@@ -239,10 +242,6 @@
     out_ref[:, 1] = second_ref[...]
 
 
-def copy_kernel(in_ref, out_ref):
-    out_ref[...] = in_ref[...]
-
-
 def on_vmem(body, shape, kinds, name, moved):
     return pl.pallas_call(
         body,
@@ -276,14 +275,13 @@
     first = next_section(first, range(owners))
     second = next_section(second, range(0, owners, 2))
     smem, vmem = pltpu.SMEM, pltpu.VMEM
-    rest = on_vmem(copy_kernel, rest.shape, [vmem], "ready_rows", 4_000_000)(rest)
     rest = lax.all_to_all(rest, "seq", split_axis=0, concat_axis=0, tiled=True)
     half = (2 * TILE, H * HD)
     done = on_vmem(place_rows, half, [smem, vmem], "place_rows", 4_000_000)(slots, rest)
+    stacked = on_vmem(stack_kernel, rest.shape, [vmem, vmem, pl.ANY], "stack_rows", 4_000_000)(
+        first, second, done
+    )
     done = next_section(done, range(owners))
-    stacked = on_vmem(stack_kernel, rest.shape, [vmem, vmem, pl.ANY], "stack_rows", 4_000_000)(
-        first, second, rest
-    )
     moved = lax.all_to_all(stacked, "seq", split_axis=0, concat_axis=0, tiled=True)
     whole = (2 * half[0], half[1])
     return on_vmem(join_kernel, whole, [smem, vmem, vmem], "join_rows", 6_000_000)(

time: 303 us -> 278 us (0.917)
  Pallas kernels: 39.9 us -> 30.8 us
  starting transfers between devices: 34.3 us -> 26.3 us
  local copies, waits for them, and re-layouts: 15.7 us -> 8.38 us
    all_to_all x1, waiting for transfers between devices: 0.01 us -> 25 us  [local(): rest = lax.all_to_all(rest, 'seq', split_axis=0, concat_axis=0, tiled=True)]
    ppermute x3, waiting for transfers between devices: 61.9 us -> 37.2 us  [next_section(): return lax.ppermute(block, ('section', 'seq'), route)]
    pallas_call x1, Pallas kernels: 29.1 us -> 15.6 us  [attend(): pl.pallas_call(attend_kernel, out_shape=(part, part, jax.ShapeDtypeStruct...]
    unnamed x24, local copies, waits for them, and re-layouts: 15.7 us -> 8.38 us
    all_to_all x1, starting transfers between devices: 12.8 us -> 5.71 us  [local(): rest = lax.all_to_all(rest, 'seq', split_axis=0, concat_axis=0, tiled=True)]
    pallas_call x1, Pallas kernels: 5.69 us -> 10 us  [pack(): pl.pallas_call(pack_kernel, out_shape=(jax.ShapeDtypeStruct((SLOTS, 3, x....]
where the time goes in v3:
time: 278 us; the launch traced here: 277 us
  blocking collectives  149 us (54%)
  waiting for transfers between devices  62.1 us (22%)
  Pallas kernels  30.8 us (11%)
  starting transfers between devices  26.3 us (9%)
  local copies, waits for them, and re-layouts  8.38 us (3%)
    all_to_all x1, blocking collectives, local(): lax.all_to_all(packed, 'seq', split_axis=0, concat_axis=0, tiled=True)  149 us
    ppermute x3, waiting for transfers between devices, next_section(): return lax.ppermute(block, ('section', 'seq'), route)  37.2 us
    all_to_all x1, waiting for transfers between devices, local(): rest = lax.all_to_all(rest, 'seq', split_axis=0, concat_axis=0, tiled=True)  25 us
    all_to_all x1, starting transfers between devices, local(): lax.all_to_all(stacked, 'seq', split_axis=0, concat_axis=0, tiled=True)  17.2 us
    pallas_call x1, Pallas kernels, attend(): pl.pallas_call(attend_kernel, out_shape=(part, part, jax.ShapeDtypeStruct...  15.6 us
    pallas_call x1, Pallas kernels, pack(): pl.pallas_call(pack_kernel, out_shape=(jax.ShapeDtypeStruct((SLOTS, 3, x....  10 us
    unnamed x24, local copies, waits for them, and re-layouts  8.38 us
    all_to_all x1, starting transfers between devices, local(): rest = lax.all_to_all(rest, 'seq', split_axis=0, concat_axis=0, tiled=True)  5.71 us
  transfers between devices with their start and end apart: 5, of which 2 were waited for; matrix products, arithmetic and copies ran while one was open for 0% of the time, Pallas kernels for 0%

profile of v3, /device:TPU:1, one launch (start us, length us, event | category | flops | bytes accessed | tf_op | source)
XLA Modules:
  0.0 277.0 jit_solution(9371981279881809472)
XLA Ops:
  0.0 10.0 %pack_heads.1 = (bf16[32,3,512,128]{3,2,1,0:T(8,128)(2,1)}, s32[40]{0:T(128)}) custom-call(s32[24,128]{1,0:T(8,128)} %counts_ref.3, bf16[3,512,3072]{2,1,0:T(8,128)(2,1)} %bitcast.8), custom_call_target="tpu_custom_call" | custom-call | bytes 25000000 | tf_op jit(solution)/shard_map/pack_heads/pallas_call | solution.py:64
  10.0 0.0 copy-start.5
  10.0 0.0 copy-start.6
  10.1 0.0 copy-start.10
  10.1 0.0 copy-start.11
  10.1 149.2 %all_to_all.15 = bf16[32,3,512,128]{3,2,1,0:T(8,128)(2,1)S(1)} all-to-all(bf16[32,3,512,128]{3,2,1,0:T(8,128)(2,1)} %get-tuple-element.11), channel_id=1, replica_groups=mesh['section'=4,'seq'=32] {'seq'}, dimensions={0} | all-to-all | bytes 25165824 | tf_op jit(solution)/shard_map/all_to_all | solution.py:271
  159.3 15.6 %attend_tiles.1 = (bf16[32,128,128]{2,1,0:T(8,128)(2,1)S(1)}, bf16[32,128,128]{2,1,0:T(8,128)(2,1)S(1)}, bf16[32,2,128,128]{3,2,1,0:T(8,128)(2,1)S(1)}) custom-call(s32[40]{0:T(128)S(1)} %copy-done.6, s32[24]{0:T(128)S(1)} %copy-done.11, s32[16,128]{1,0:T(8,128)S(1)} %bitcast.7, s32[24,128]{1,0:T(8,128)S(1)} %copy-done.5, bf16[1,3072]{1,0:T(2,128)(2,1)S(1)} %copy-done.9, ...), custom_call_target="tpu_custom_call" | custom-call | flops 20000000000 | bytes 17000000 | tf_op jit(solution)/shard_map/attend_tiles/pallas_call | solution.py:200
  175.0 1.3 copy-done.2
  176.3 1.0 copy-done.7
  177.3 1.0 copy-done.8
  178.3 5.7 %all-to-all-start.1 = ((bf16[32,2,128,128]{3,2,1,0:T(8,128)(2,1)}), bf16[32,2,128,128]{3,2,1,0:T(8,128)(2,1)S(1)}, u32[]{:S(2)}, u32[]{:S(2)}) async-start(bf16[32,2,128,128]{3,2,1,0:T(8,128)(2,1)} %copy-done.2), calls=%async_computation.1 | async-start | bytes 4194304 | tf_op jit(solution)/shard_map/all_to_all | solution.py:278
  184.0 1.7 collective-permute-start
  185.7 1.6 collective-permute-start.1
  187.3 25.0 %all-to-all-done.1.rows_ref = bf16[32,2,128,128]{3,2,1,0:T(8,128)(2,1)S(1)} async-done(((bf16[32,2,128,128]{3,2,1,0:T(8,128)(2,1)}), bf16[32,2,128,128]{3,2,1,0:T(8,128)(2,1)S(1)}, u32[]{:S(2)}, u32[]{:S(2)}) %all-to-all-start.1) | async-done | bytes 2097184 | tf_op jit(solution)/shard_map/all_to_all | solution.py:278
  212.3 1.0 place_rows.1.after_ref
  213.3 1.4 stack_rows.1
  214.7 1.3 copy-done
  216.0 1.2 copy-done.1
  217.2 17.2 %all-to-all-start.2 = ((bf16[32,2,128,128]{3,2,1,0:T(8,128)(2,1)}), bf16[32,2,128,128]{3,2,1,0:T(8,128)(2,1)S(1)}, u32[]{:S(2)}, u32[]{:S(2)}) async-start(bf16[32,2,128,128]{3,2,1,0:T(8,128)(2,1)} %copy-done), calls=%async_computation.2 | async-start | bytes 4194304 | tf_op jit(solution)/shard_map/all_to_all | solution.py:285
  234.4 0.1 collective-permute-start.2
  234.4 37.2 %collective-permute-done.2.done_ref = bf16[256,3072]{1,0:T(8,128)(2,1)S(1)} collective-permute-done((bf16[256,3072]{1,0:T(8,128)(2,1)}, bf16[256,3072]{1,0:T(8,128)(2,1)S(1)}, u32[]{:S(2)}, u32[]{:S(2)}) %collective-permute-start.2) | collective-permute-done | bytes 1572896 | tf_op jit(solution)/shard_map/ppermute | solution.py:265
  271.6 1.2 copy-done.3
  272.8 1.4 copy-done.4
  274.2 2.8 %join_rows.1 = bf16[512,3072]{1,0:T(8,128)(2,1)} custom-call(s32[40]{0:T(128)S(1)} %copy-done.6, bf16[32,2,128,128]{3,2,1,0:T(8,128)(2,1)S(1)} %all-to-all-done.2.rows_ref, bf16[256,3072]{1,0:T(8,128)(2,1)S(1)} %copy-done.4), custom_call_target="tpu_custom_call" | custom-call | bytes 6000000 | tf_op jit(solution)/shard_map/join_rows/pallas_call | solution.py:287
  (16 shorter events, 0.0 us)
Async XLA Ops:
  10.0 149.3 %copy-start.5 = (s32[24,128]{1,0:T(8,128)S(1)}, s32[24,128]{1,0:T(8,128)}, u32[]{:S(2)}) copy-start(s32[24,128]{1,0:T(8,128)} %counts_ref.3) | copy-start | bytes 36868
  10.0 149.3 %copy-start.6 = (s32[40]{0:T(128)S(1)}, s32[40]{0:T(128)}, u32[]{:S(2)}) copy-start(s32[40]{0:T(128)} %get-tuple-element.10.slot_ref) | copy-start | bytes 484
  10.0 149.3 %copy-start.9 = (bf16[1,3072]{1,0:T(2,128)(2,1)S(1)}, bf16[1,3072]{1,0:T(2,128)(2,1)}, u32[]{:S(2)}) copy-start(bf16[1,3072]{1,0:T(2,128)(2,1)} %gate_ref.1) | copy-start | bytes 18436
  10.1 149.3 %copy-start.10 = (s32[2,128,8]{1,2,0:T(8,128)S(1)}, s32[2,128,8]{1,2,0:T(8,128)}, u32[]{:S(2)}) copy-start(s32[2,128,8]{1,2,0:T(8,128)} %param.8) | copy-start | bytes 24580
  10.1 149.3 %copy-start.11 = (s32[24]{0:T(128)S(1)}, s32[24]{0:T(128)}, u32[]{:S(2)}) copy-start(s32[24]{0:T(128)} %class_ref.1) | copy-start | bytes 292
  175.0 1.3 copy-start.2
  176.3 1.0 copy-start.7
  177.3 1.0 copy-start.8
  178.3 34.0 %all-to-all-start.1 = ((bf16[32,2,128,128]{3,2,1,0:T(8,128)(2,1)}), bf16[32,2,128,128]{3,2,1,0:T(8,128)(2,1)S(1)}, u32[]{:S(2)}, u32[]{:S(2)}) async-start(bf16[32,2,128,128]{3,2,1,0:T(8,128)(2,1)} %copy-done.2), calls=%async_computation.1 | async-start | bytes 4194304 | tf_op jit(solution)/shard_map/all_to_all | solution.py:278
  184.0 29.3 %collective-permute-start = (bf16[32,128,128]{2,1,0:T(8,128)(2,1)}, bf16[32,128,128]{2,1,0:T(8,128)(2,1)S(1)}, u32[]{:S(2)}, u32[]{:S(2)}) collective-permute-start(bf16[32,128,128]{2,1,0:T(8,128)(2,1)} %copy-done.8), channel_id=1, source_target_pairs={{0,32},{1,33},{2,34},{3,35},{4,36},{5,37},{6,38},{7,39},{8,40},{9,... | collective-permute-start | bytes 3145736 | tf_op jit(solution)/shard_map/ppermute | solution.py:265
  185.7 27.6 %collective-permute-start.1 = (bf16[32,128,128]{2,1,0:T(8,128)(2,1)}, bf16[32,128,128]{2,1,0:T(8,128)(2,1)}, u32[]{:S(2)}, u32[]{:S(2)}) collective-permute-start(bf16[32,128,128]{2,1,0:T(8,128)(2,1)} %copy-done.7), channel_id=1, source_target_pairs={{0,32},{2,34},{4,36},{6,38},{8,40},{10,42},{12,44},{14,46},{16,48}... | collective-permute-start | bytes 3145736 | tf_op jit(solution)/shard_map/ppermute | solution.py:265
  214.7 1.3 copy-start
  216.0 1.2 copy-start.1
  217.2 55.6 %all-to-all-start.2 = ((bf16[32,2,128,128]{3,2,1,0:T(8,128)(2,1)}), bf16[32,2,128,128]{3,2,1,0:T(8,128)(2,1)S(1)}, u32[]{:S(2)}, u32[]{:S(2)}) async-start(bf16[32,2,128,128]{3,2,1,0:T(8,128)(2,1)} %copy-done), calls=%async_computation.2 | async-start | bytes 4194304 | tf_op jit(solution)/shard_map/all_to_all | solution.py:285
  234.4 37.3 %collective-permute-start.2 = (bf16[256,3072]{1,0:T(8,128)(2,1)}, bf16[256,3072]{1,0:T(8,128)(2,1)S(1)}, u32[]{:S(2)}, u32[]{:S(2)}) collective-permute-start(bf16[256,3072]{1,0:T(8,128)(2,1)} %copy-done.1), channel_id=1, source_target_pairs={{0,32},{1,33},{2,34},{3,35},{4,36},{5,37},{6,38},{7,39},{8,40},{9,... | collective-permute-start | bytes 4718600 | tf_op jit(solution)/shard_map/ppermute | solution.py:265
  271.6 1.2 copy-start.3
  272.8 1.4 copy-start.4

commit v4 on v3

--- a/solution.py
+++ b/solution.py
@@ -13,6 +13,8 @@
 PAIRS = 32
 CHIPS = 16
 SLOTS = 2 * CHIPS
+SPARE = 1
+LONG = 2_000_000_000
 LOG2E = 1.4426950408889634
 
 
@@ -83,10 +85,11 @@
 
 def attend_kernel(
     slot_ref, class_ref, lists_ref, counts_ref, gate_ref, x_ref,
-    first_ref, second_ref, rest_ref,
+    pair_ref, single_ref, rest_ref,
     held, result, sorted_ref, start_ref, in_sems, out_sems,
 ):
     pieces = in_sems.shape[0]
+    owners = x_ref.shape[0]
     width = x_ref.shape[0] // pieces
     loads = [
         pltpu.make_async_copy(
@@ -181,10 +184,11 @@
         lax.fori_loop(0, (end - begin + group - 1) // group, unit, 0)
 
     stores = [
-        pltpu.make_async_copy(result.at[0], first_ref, out_sems.at[0]),
-        pltpu.make_async_copy(result.at[1], second_ref, out_sems.at[1]),
+        pltpu.make_async_copy(result.at[0], pair_ref.at[pl.ds(0, owners), 0], out_sems.at[0]),
+        pltpu.make_async_copy(result.at[1], pair_ref.at[pl.ds(0, owners), 1], out_sems.at[1]),
         pltpu.make_async_copy(result.at[2], rest_ref.at[:, 0], out_sems.at[2]),
         pltpu.make_async_copy(result.at[3], rest_ref.at[:, 1], out_sems.at[3]),
+        pltpu.make_async_copy(result.at[0], single_ref, out_sems.at[4]),
     ]
     for store in stores:
         store.start()
@@ -197,9 +201,10 @@
     smem = pl.BlockSpec(memory_space=pltpu.SMEM)
     anywhere = pl.BlockSpec(memory_space=pl.ANY)
     part = jax.ShapeDtypeStruct((owners, TILE, HD), jnp.bfloat16)
+    pair = jax.ShapeDtypeStruct((owners + SPARE, 2, TILE, HD), jnp.bfloat16)
     return pl.pallas_call(
         attend_kernel,
-        out_shape=(part, part, jax.ShapeDtypeStruct((owners, 2, TILE, HD), jnp.bfloat16)),
+        out_shape=(pair, part, jax.ShapeDtypeStruct((owners, 2, TILE, HD), jnp.bfloat16)),
         in_specs=[smem, smem, smem, smem, pl.BlockSpec(memory_space=pltpu.VMEM), anywhere],
         out_specs=(anywhere, anywhere, anywhere),
         scratch_shapes=[
@@ -208,9 +213,9 @@
             pltpu.SMEM((owners * 4,), jnp.int32),
             pltpu.SMEM((KMAX + 2,), jnp.int32),
             pltpu.SemaphoreType.DMA((8,)),
-            pltpu.SemaphoreType.DMA((4,)),
+            pltpu.SemaphoreType.DMA((5,)),
         ],
-        compiler_params=pltpu.CompilerParams(vmem_limit_bytes=32 * 1024 * 1024),
+        compiler_params=pltpu.CompilerParams(vmem_limit_bytes=60 * 1024 * 1024),
         cost_estimate=pl.CostEstimate(
             flops=20_000_000_000, bytes_accessed=17_000_000, transcendentals=8_000_000
         ),
@@ -231,26 +236,47 @@
     lax.fori_loop(0, CHIPS, one_chip, 0)
 
 
-def join_kernel(slot_ref, rows_ref, done_ref, out_ref):
-    place_rows(slot_ref, rows_ref, out_ref)
+def stack_kernel(pair_ref, single_ref, out_ref):
+    shared = lax.rem(lax.axis_index("seq"), 2)
+    owners = single_ref.shape[0]
+
+    @pl.when(shared == 0)
+    def _():
+        out_ref[...] = pair_ref[:owners]
+
+    @pl.when(shared == 1)
+    def _():
+        out_ref[:, 0] = single_ref[...]
+
+
+def after_kernel(in_ref, before_ref, out_ref):
+    pass
+
+
+def lay_kernel(done_ref, out_ref, sem):
     half = done_ref.shape[0]
-    out_ref[half:, :] = done_ref[...]
-
-
-def stack_kernel(first_ref, second_ref, after_ref, out_ref):
-    out_ref[:, 0] = first_ref[...]
-    out_ref[:, 1] = second_ref[...]
-
-
-def on_vmem(body, shape, kinds, name, moved):
+    copy = pltpu.make_async_copy(done_ref, out_ref.at[pl.ds(half, half)], sem)
+    copy.start()
+    copy.wait()
+
+
+def join_kernel(slot_ref, rows_ref, laid_ref, out_ref, half_ref, sem):
+    place_rows(slot_ref, rows_ref, half_ref)
+    copy = pltpu.make_async_copy(half_ref, out_ref.at[pl.ds(0, half_ref.shape[0])], sem)
+    copy.start()
+    copy.wait()
+
+
+def small_call(body, shape, kinds, name, cost=4_000_000, kind=pltpu.VMEM, **more):
     return pl.pallas_call(
         body,
         out_shape=jax.ShapeDtypeStruct(shape, jnp.bfloat16),
-        in_specs=[pl.BlockSpec(memory_space=kind) for kind in kinds],
-        out_specs=pl.BlockSpec(memory_space=pltpu.VMEM),
-        compiler_params=pltpu.CompilerParams(vmem_limit_bytes=32 * 1024 * 1024),
-        cost_estimate=pl.CostEstimate(flops=0, bytes_accessed=moved, transcendentals=0),
+        in_specs=[pl.BlockSpec(memory_space=k) for k in kinds],
+        out_specs=pl.BlockSpec(memory_space=kind),
+        compiler_params=pltpu.CompilerParams(vmem_limit_bytes=60 * 1024 * 1024),
+        cost_estimate=pl.CostEstimate(flops=cost * 10000 if cost > 1e8 else 0, bytes_accessed=cost, transcendentals=0),
         name=name,
+        **more,
     )
 
 
@@ -271,22 +297,29 @@
     arrived = lax.all_to_all(packed, "seq", split_axis=0, concat_axis=0, tiled=True)
     arrived = arrived.reshape(owners, 3, 4, TILE, HD)
     lists = tile_lists.transpose(0, 2, 1).reshape(-1, tile_lists.shape[1])
-    first, second, rest = attend(slots, head_class, lists, tile_counts, gate, arrived)
-    first = next_section(first, range(owners))
-    second = next_section(second, range(0, owners, 2))
+    pair, single, rest = attend(slots, head_class, lists, tile_counts, gate, arrived)
+    pair = next_section(pair, range(0, owners, 2))
+    single = next_section(single, range(1, owners, 2))
     smem, vmem = pltpu.SMEM, pltpu.VMEM
+    stacked = small_call(stack_kernel, rest.shape, [vmem, vmem], "stack_rows", LONG)(pair, single)
     rest = lax.all_to_all(rest, "seq", split_axis=0, concat_axis=0, tiled=True)
     half = (2 * TILE, H * HD)
-    done = on_vmem(place_rows, half, [smem, vmem], "place_rows", 4_000_000)(slots, rest)
-    stacked = on_vmem(stack_kernel, rest.shape, [vmem, vmem, pl.ANY], "stack_rows", 4_000_000)(
-        first, second, done
-    )
+    done = small_call(place_rows, half, [smem, vmem], "place_rows",1000)(slots, rest)
+    stacked = small_call(
+        after_kernel, rest.shape, [pl.ANY, pl.ANY], "rows_after", 1000, pl.ANY,
+        input_output_aliases={0: 0},
+    )(stacked, done)
     done = next_section(done, range(owners))
+    whole = (2 * half[0], half[1])
+    dma = pltpu.SemaphoreType.DMA
+    laid = small_call(
+        lay_kernel, whole, [vmem], "lay_rows", LONG, pl.ANY, scratch_shapes=[dma]
+    )(done)
     moved = lax.all_to_all(stacked, "seq", split_axis=0, concat_axis=0, tiled=True)
-    whole = (2 * half[0], half[1])
-    return on_vmem(join_kernel, whole, [smem, vmem, vmem], "join_rows", 6_000_000)(
-        slots, moved, done
-    )[None]
+    return small_call(
+        join_kernel, whole, [smem, vmem, pl.ANY], "join_rows", kind=pl.ANY,
+        input_output_aliases={2: 0}, scratch_shapes=[vmem(half, jnp.bfloat16), dma],
+    )(slots, moved, laid)[None]
 
 
 def solution(mesh):

time: 278 us -> 264 us (0.950)
  Pallas kernels: 30.8 us -> 43.1 us
  waiting for transfers between devices: 62.1 us -> 50.8 us
  starting transfers between devices: 26.3 us -> 18.5 us
  local copies, waits for them, and re-layouts: 8.38 us -> 1.33 us
    pallas_call x4 -> x6, Pallas kernels: 20.8 us -> 33 us  [the longest x1 20.7 us: attend(): pl.pallas_call(attend_kernel, out_shape=(pair, part, jax.ShapeDtypeStruct...]
    all_to_all x1, starting transfers between devices: 17.2 us -> 5.56 us  [local(): lax.all_to_all(stacked, 'seq', split_axis=0, concat_axis=0, tiled=True)]
    ppermute x3, waiting for transfers between devices: 37.2 us -> 26.1 us  [next_section(): return lax.ppermute(block, ('section', 'seq'), route)]
    unnamed x24 -> x4, local copies, waits for them, and re-layouts: 8.38 us -> 1.33 us
    ppermute x3, starting transfers between devices: 3.41 us -> 7.34 us  [next_section(): return lax.ppermute(block, ('section', 'seq'), route)]
  transfers between devices with their start and end apart: 5 -> 5, of which waited for: 2 -> 2; matrix products, arithmetic and copies ran while one was open for 0% -> 0% of each run, Pallas kernels for 0% -> 3%
where the time goes in v4:
time: 264 us; the launch traced here: 263 us
  blocking collectives  149 us (56%)
  waiting for transfers between devices  50.8 us (19%)
  Pallas kernels  43.1 us (16%)
  starting transfers between devices  18.5 us (7%)
    all_to_all x1, blocking collectives, local(): lax.all_to_all(packed, 'seq', split_axis=0, concat_axis=0, tiled=True)  149 us
    ppermute x3, waiting for transfers between devices, next_section(): return lax.ppermute(block, ('section', 'seq'), route)  26.1 us
    all_to_all x1, waiting for transfers between devices, local(): rest = lax.all_to_all(rest, 'seq', split_axis=0, concat_axis=0, tiled=True)  24.7 us
    pallas_call x1, Pallas kernels, attend(): pl.pallas_call(attend_kernel, out_shape=(pair, part, jax.ShapeDtypeStruct...  20.7 us
    pallas_call x1, Pallas kernels, pack(): pl.pallas_call(pack_kernel, out_shape=(jax.ShapeDtypeStruct((SLOTS, 3, x....  10.1 us
    ppermute x3, starting transfers between devices, next_section(): return lax.ppermute(block, ('section', 'seq'), route)  7.34 us
    all_to_all x1, starting transfers between devices, local(): lax.all_to_all(stacked, 'seq', split_axis=0, concat_axis=0, tiled=True)  5.56 us
    all_to_all x1, starting transfers between devices, local(): rest = lax.all_to_all(rest, 'seq', split_axis=0, concat_axis=0, tiled=True)  5.56 us
  transfers between devices with their start and end apart: 5, of which 2 were waited for; matrix products, arithmetic and copies ran while one was open for 0% of the time, Pallas kernels for 3%

profile of v4, /device:TPU:1, one launch (start us, length us, event | category | flops | bytes accessed | tf_op | source)
XLA Modules:
  0.0 263.0 jit_solution(9268068687107771619)
XLA Ops:
  0.0 10.1 %pack_heads.1 = (bf16[32,3,512,128]{3,2,1,0:T(8,128)(2,1)}, s32[40]{0:T(128)}) custom-call(s32[24,128]{1,0:T(8,128)} %counts_ref.3, bf16[3,512,3072]{2,1,0:T(8,128)(2,1)} %bitcast.7), custom_call_target="tpu_custom_call" | custom-call | bytes 25000000 | tf_op jit(solution)/shard_map/pack_heads/pallas_call | solution.py:66
  10.1 149.2 %all_to_all.15 = bf16[32,3,512,128]{3,2,1,0:T(8,128)(2,1)} all-to-all(bf16[32,3,512,128]{3,2,1,0:T(8,128)(2,1)} %get-tuple-element.11), channel_id=1, replica_groups=mesh['section'=4,'seq'=32] {'seq'}, dimensions={0} | all-to-all | bytes 25165824 | tf_op jit(solution)/shard_map/all_to_all | solution.py:297
  159.3 20.7 %attend_tiles.1 = (bf16[33,2,128,128]{3,2,1,0:T(8,128)(2,1)}, bf16[32,128,128]{2,1,0:T(8,128)(2,1)}, bf16[32,2,128,128]{3,2,1,0:T(8,128)(2,1)}) custom-call(s32[40]{0:T(128)} %get-tuple-element.10.slot_ref, s32[24]{0:T(128)} %class_ref.1, s32[16,128]{1,0:T(8,128)} %bitcast.8, s32[24,128]{1,0:T(8,128)} %counts_ref.3, bf16[1,3072]{1,0:T(2,128)(2,1)} %gate_ref.1, ...), custom_call_target="tpu_custom_call" | custom-call | flops 20000000000 | bytes 17000000 | tf_op jit(solution)/shard_map/attend_tiles/pallas_call | solution.py:205
  180.0 0.0 copy-start.1
  180.0 2.2 collective-permute-start
  182.2 5.6 %all-to-all-start.1 = ((bf16[32,2,128,128]{3,2,1,0:T(8,128)(2,1)}), bf16[32,2,128,128]{3,2,1,0:T(8,128)(2,1)S(1)}, u32[]{:S(2)}, u32[]{:S(2)}) async-start(bf16[32,2,128,128]{3,2,1,0:T(8,128)(2,1)} %get-tuple-element.14), calls=%async_computation.1 | async-start | bytes 4194304 | tf_op jit(solution)/shard_map/all_to_all | solution.py:305
  187.8 0.0 copy-done.1
  187.8 3.5 %collective-permute-start.1 = (bf16[32,128,128]{2,1,0:T(8,128)(2,1)S(1)}, bf16[32,128,128]{2,1,0:T(8,128)(2,1)}, u32[]{:S(2)}, u32[]{:S(2)}) collective-permute-start(bf16[32,128,128]{2,1,0:T(8,128)(2,1)S(1)} %copy-done.1), channel_id=1, source_target_pairs={{1,33},{3,35},{5,37},{7,39},{9,41},{11,43},{13,45},{15,47},{17,49}... | collective-permute-start | bytes 3145736 | tf_op jit(solution)/shard_map/ppermute | solution.py:291
  191.3 24.7 %all-to-all-done.1.rows_ref = bf16[32,2,128,128]{3,2,1,0:T(8,128)(2,1)S(1)} async-done(((bf16[32,2,128,128]{3,2,1,0:T(8,128)(2,1)}), bf16[32,2,128,128]{3,2,1,0:T(8,128)(2,1)S(1)}, u32[]{:S(2)}, u32[]{:S(2)}) %all-to-all-start.1) | async-done | bytes 2097184 | tf_op jit(solution)/shard_map/all_to_all | solution.py:305
  216.1 0.0 copy-start
  216.1 1.3 copy-done
  217.4 3.3 %place_rows.1.before_ref = bf16[256,3072]{1,0:T(8,128)(2,1)} custom-call(s32[40]{0:T(128)} %get-tuple-element.10.slot_ref, bf16[32,2,128,128]{3,2,1,0:T(8,128)(2,1)} %copy-done), custom_call_target="tpu_custom_call" | custom-call | bytes 1000 | tf_op jit(solution)/shard_map/place_rows/pallas_call | solution.py:307
  220.6 1.6 collective-permute-start.2
  222.3 0.0 collective-permute-done.1.single_ref
  222.3 0.0 collective-permute-done.pair_ref
  222.3 3.3 %stack_rows.1.in_ref = bf16[32,2,128,128]{3,2,1,0:T(8,128)(2,1)} custom-call(bf16[33,2,128,128]{3,2,1,0:T(8,128)(2,1)} %collective-permute-done.pair_ref, bf16[32,128,128]{2,1,0:T(8,128)(2,1)} %collective-permute-done.1.single_ref), custom_call_target="tpu_custom_call" | custom-call | flops 19999999655936 | bytes 2000000000 | tf_op jit(solution)/shard_map/stack_rows/pallas_call | solution.py:304
  225.5 5.6 %all-to-all-start.2 = ((bf16[32,2,128,128]{3,2,1,0:T(8,128)(2,1)}), bf16[32,2,128,128]{3,2,1,0:T(8,128)(2,1)}, u32[]{:S(2)}, u32[]{:S(2)}) async-start(bf16[32,2,128,128]{3,2,1,0:T(8,128)(2,1)} %rows_after.1), calls=%async_computation.2 | async-start | bytes 4194304 | tf_op jit(solution)/shard_map/all_to_all | solution.py:318
  231.1 26.1 %collective-permute-done.2.done_ref = bf16[256,3072]{1,0:T(8,128)(2,1)} collective-permute-done((bf16[256,3072]{1,0:T(8,128)(2,1)}, bf16[256,3072]{1,0:T(8,128)(2,1)}, u32[]{:S(2)}, u32[]{:S(2)}) %collective-permute-start.2) | collective-permute-done | bytes 1572896 | tf_op jit(solution)/shard_map/ppermute | solution.py:291
  257.2 2.6 lay_rows.1.laid_ref
  259.8 0.0 all-to-all-done.2.rows_ref
  259.8 3.2 %join_rows.1 = bf16[512,3072]{1,0:T(8,128)(2,1)} custom-call(s32[40]{0:T(128)} %get-tuple-element.10.slot_ref, bf16[32,2,128,128]{3,2,1,0:T(8,128)(2,1)} %all-to-all-done.2.rows_ref, bf16[512,3072]{1,0:T(8,128)(2,1)} %lay_rows.1.laid_ref), custom_call_target="tpu_custom_call", output_to_operand_aliasing={{}: (2, {})} | custom-call | bytes 4000000 | tf_op jit(solution)/shard_map/join_rows/pallas_call | solution.py:319
  (1 shorter events, 0.0 us)
Async XLA Ops:
  180.0 7.7 %copy-start.1 = (bf16[32,128,128]{2,1,0:T(8,128)(2,1)S(1)}, bf16[32,128,128]{2,1,0:T(8,128)(2,1)}, u32[]{:S(2)}) copy-start(bf16[32,128,128]{2,1,0:T(8,128)(2,1)} %get-tuple-element.13) | copy-start | bytes 3145732
  180.0 42.2 %collective-permute-start = (bf16[33,2,128,128]{3,2,1,0:T(8,128)(2,1)}, bf16[33,2,128,128]{3,2,1,0:T(8,128)(2,1)}, u32[]{:S(2)}, u32[]{:S(2)}) collective-permute-start(bf16[33,2,128,128]{3,2,1,0:T(8,128)(2,1)} %get-tuple-element.12), channel_id=1, source_target_pairs={{0,32},{2,34},{4,36},{6,38},{8,40},{10,42},{12,44},{14,46},{16,48}... | collective-permute-start | bytes 6488072 | tf_op jit(solution)/shard_map/ppermute | solution.py:291
  182.2 33.9 %all-to-all-start.1 = ((bf16[32,2,128,128]{3,2,1,0:T(8,128)(2,1)}), bf16[32,2,128,128]{3,2,1,0:T(8,128)(2,1)S(1)}, u32[]{:S(2)}, u32[]{:S(2)}) async-start(bf16[32,2,128,128]{3,2,1,0:T(8,128)(2,1)} %get-tuple-element.14), calls=%async_computation.1 | async-start | bytes 4194304 | tf_op jit(solution)/shard_map/all_to_all | solution.py:305
  187.8 34.5 %collective-permute-start.1 = (bf16[32,128,128]{2,1,0:T(8,128)(2,1)S(1)}, bf16[32,128,128]{2,1,0:T(8,128)(2,1)}, u32[]{:S(2)}, u32[]{:S(2)}) collective-permute-start(bf16[32,128,128]{2,1,0:T(8,128)(2,1)S(1)} %copy-done.1), channel_id=1, source_target_pairs={{1,33},{3,35},{5,37},{7,39},{9,41},{11,43},{13,45},{15,47},{17,49}... | collective-permute-start | bytes 3145736 | tf_op jit(solution)/shard_map/ppermute | solution.py:291
  216.1 1.3 copy-start
  220.6 36.6 %collective-permute-start.2 = (bf16[256,3072]{1,0:T(8,128)(2,1)}, bf16[256,3072]{1,0:T(8,128)(2,1)}, u32[]{:S(2)}, u32[]{:S(2)}) collective-permute-start(bf16[256,3072]{1,0:T(8,128)(2,1)} %place_rows.1.before_ref), channel_id=1, source_target_pairs={{0,32},{1,33},{2,34},{3,35},{4,36},{5,37},{6,38},{7,39},{8,40},{9,... | collective-permute-start | bytes 4718600 | tf_op jit(solution)/shard_map/ppermute | solution.py:291
  225.5 34.2 %all-to-all-start.2 = ((bf16[32,2,128,128]{3,2,1,0:T(8,128)(2,1)}), bf16[32,2,128,128]{3,2,1,0:T(8,128)(2,1)}, u32[]{:S(2)}, u32[]{:S(2)}) async-start(bf16[32,2,128,128]{3,2,1,0:T(8,128)(2,1)} %rows_after.1), calls=%async_computation.2 | async-start | bytes 4194304 | tf_op jit(solution)/shard_map/all_to_all | solution.py:318

commit v5 on v4

--- a/solution.py
+++ b/solution.py
@@ -13,8 +13,7 @@
 PAIRS = 32
 CHIPS = 16
 SLOTS = 2 * CHIPS
-SPARE = 1
-LONG = 2_000_000_000
+LONG = 20_000_000_000_000
 LOG2E = 1.4426950408889634
 
 
@@ -183,17 +182,21 @@
 
         lax.fori_loop(0, (end - begin + group - 1) // group, unit, 0)
 
-    stores = [
-        pltpu.make_async_copy(result.at[0], pair_ref.at[pl.ds(0, owners), 0], out_sems.at[0]),
-        pltpu.make_async_copy(result.at[1], pair_ref.at[pl.ds(0, owners), 1], out_sems.at[1]),
-        pltpu.make_async_copy(result.at[2], rest_ref.at[:, 0], out_sems.at[2]),
-        pltpu.make_async_copy(result.at[3], rest_ref.at[:, 1], out_sems.at[3]),
-        pltpu.make_async_copy(result.at[0], single_ref, out_sems.at[4]),
-    ]
-    for store in stores:
-        store.start()
-    for store in stores:
-        store.wait()
+    sends = [
+        (0, pair_ref.at[pl.ds(0, owners), 0], 0),
+        (1, pair_ref.at[pl.ds(0, owners), 1], 0),
+        (3, rest_ref.at[:, 1], 0),
+        (0, single_ref, 1),
+        (2, rest_ref.at[:, 0], None),
+    ]
+    for wait in (False, True):
+        for n, (row, target, only) in enumerate(sends):
+            store = pltpu.make_async_copy(result.at[row], target, out_sems.at[n])
+            act = store.wait if wait else store.start
+            if only is None:
+                act()
+            else:
+                pl.when(shared == only)(act)
 
 
 def attend(slots, head_class, lists, counts, gate, arrived):
@@ -201,7 +204,7 @@
     smem = pl.BlockSpec(memory_space=pltpu.SMEM)
     anywhere = pl.BlockSpec(memory_space=pl.ANY)
     part = jax.ShapeDtypeStruct((owners, TILE, HD), jnp.bfloat16)
-    pair = jax.ShapeDtypeStruct((owners + SPARE, 2, TILE, HD), jnp.bfloat16)
+    pair = jax.ShapeDtypeStruct((owners, 2, TILE, HD), jnp.bfloat16)
     return pl.pallas_call(
         attend_kernel,
         out_shape=(pair, part, jax.ShapeDtypeStruct((owners, 2, TILE, HD), jnp.bfloat16)),
@@ -223,58 +226,102 @@
     )(slots, head_class, lists, counts, gate, arrived)
 
 
-def place_rows(slot_ref, rows_ref, out_ref):
-    def one_chip(chip, carry):
-        columns = pl.ds(pl.multiple_of(slot_ref[2 * chip] * HD, HD), HD)
-        for i in range(2):
-            out_ref[i * TILE : (i + 1) * TILE, columns] = rows_ref[2 * chip, i]
-        columns = pl.ds(pl.multiple_of(slot_ref[2 * chip + 1] * HD, HD), HD)
-        start = pl.multiple_of(chip // SHARED * TILE, TILE)
-        out_ref[pl.ds(start, TILE), columns] = rows_ref[2 * chip + 1, 0]
-        return carry
-
-    lax.fori_loop(0, CHIPS, one_chip, 0)
-
-
-def stack_kernel(pair_ref, single_ref, out_ref):
-    shared = lax.rem(lax.axis_index("seq"), 2)
-    owners = single_ref.shape[0]
-
-    @pl.when(shared == 0)
+def place_rows(slot_ref, rows_ref, out_ref, held, half, in_sems, out_sems):
+    pieces = in_sems.shape[0]
+    width, chips = rows_ref.shape[0] // pieces, CHIPS // pieces
+    loads = [
+        pltpu.make_async_copy(
+            rows_ref.at[pl.ds(n * width, width)], held.at[pl.ds(n * width, width)], in_sems.at[n]
+        )
+        for n in range(pieces)
+    ]
+    for load in loads:
+        load.start()
+    for n in range(pieces):
+        loads[n].wait()
+
+        def one_chip(i, carry, n=n):
+            chip = n * chips + i
+            columns = pl.ds(pl.multiple_of(slot_ref[2 * chip] * HD, HD), HD)
+            half[:TILE, columns] = held[2 * chip, 0]
+            half[TILE:, columns] = held[2 * chip, 1]
+            columns = pl.ds(pl.multiple_of(slot_ref[2 * chip + 1] * HD, HD), HD)
+            start = pl.multiple_of(chip // SHARED * TILE, TILE)
+            half[pl.ds(start, TILE), columns] = held[2 * chip + 1, 0]
+            return carry
+
+        lax.fori_loop(0, chips, one_chip, 0)
+    return send_rows(half, out_ref, out_sems)
+
+
+def send_rows(source, target, sems):
+    pieces = sems.shape[0]
+    rows = source.shape[0] // pieces
+    copies = [
+        pltpu.make_async_copy(
+            source.at[pl.ds(n * rows, rows)], target.at[pl.ds(n * rows, rows)], sems.at[n]
+        )
+        for n in range(pieces)
+    ]
+    for copy in copies:
+        copy.start()
+    return copies
+
+
+def place_kernel(slot_ref, rows_ref, out_ref, held, half, in_sems, out_sems):
+    for copy in place_rows(slot_ref, rows_ref, out_ref, held, half, in_sems, out_sems):
+        copy.wait()
+
+
+def join_kernel(
+    slot_ref, rows_ref, done_ref, out_ref, held, half, in_sems, out_sems, other, other_sems
+):
+    arrivals = send_rows(done_ref, other, other_sems.at[0])
+    rows = half.shape[0]
+    copies = place_rows(slot_ref, rows_ref, out_ref, held, half, in_sems, out_sems)
+    for arrival in arrivals:
+        arrival.wait()
+    copies += send_rows(other, out_ref.at[pl.ds(rows, rows)], other_sems.at[1])
+    for copy in copies:
+        copy.wait()
+
+
+def stack_kernel(pair_ref, single_ref, out_ref, held, in_sems, out_sems):
+    @pl.when(lax.rem(lax.axis_index("seq"), 2) == 1)
     def _():
-        out_ref[...] = pair_ref[:owners]
-
-    @pl.when(shared == 1)
-    def _():
-        out_ref[:, 0] = single_ref[...]
+        arrivals = send_rows(single_ref, held, in_sems)
+        for arrival in arrivals:
+            arrival.wait()
+        pieces = out_sems.shape[0]
+        rows = held.shape[0] // pieces
+        copies = [
+            pltpu.make_async_copy(
+                held.at[pl.ds(n * rows, rows)], out_ref.at[pl.ds(n * rows, rows), 0], out_sems.at[n]
+            )
+            for n in range(pieces)
+        ]
+        for copy in copies:
+            copy.start()
+        for copy in copies:
+            copy.wait()
 
 
 def after_kernel(in_ref, before_ref, out_ref):
     pass
 
 
-def lay_kernel(done_ref, out_ref, sem):
-    half = done_ref.shape[0]
-    copy = pltpu.make_async_copy(done_ref, out_ref.at[pl.ds(half, half)], sem)
-    copy.start()
-    copy.wait()
-
-
-def join_kernel(slot_ref, rows_ref, laid_ref, out_ref, half_ref, sem):
-    place_rows(slot_ref, rows_ref, half_ref)
-    copy = pltpu.make_async_copy(half_ref, out_ref.at[pl.ds(0, half_ref.shape[0])], sem)
-    copy.start()
-    copy.wait()
-
-
-def small_call(body, shape, kinds, name, cost=4_000_000, kind=pltpu.VMEM, **more):
+def same_kernel(in_ref, out_ref):
+    pass
+
+
+def small_call(body, shape, kinds, name, kind=pl.ANY, flops=0, **more):
     return pl.pallas_call(
         body,
         out_shape=jax.ShapeDtypeStruct(shape, jnp.bfloat16),
         in_specs=[pl.BlockSpec(memory_space=k) for k in kinds],
         out_specs=pl.BlockSpec(memory_space=kind),
         compiler_params=pltpu.CompilerParams(vmem_limit_bytes=60 * 1024 * 1024),
-        cost_estimate=pl.CostEstimate(flops=cost * 10000 if cost > 1e8 else 0, bytes_accessed=cost, transcendentals=0),
+        cost_estimate=pl.CostEstimate(flops=flops, bytes_accessed=1000, transcendentals=0),
         name=name,
         **more,
     )
@@ -300,26 +347,30 @@
     pair, single, rest = attend(slots, head_class, lists, tile_counts, gate, arrived)
     pair = next_section(pair, range(0, owners, 2))
     single = next_section(single, range(1, owners, 2))
-    smem, vmem = pltpu.SMEM, pltpu.VMEM
-    stacked = small_call(stack_kernel, rest.shape, [vmem, vmem], "stack_rows", LONG)(pair, single)
+    smem, vmem, dma = pltpu.SMEM, pltpu.VMEM, pltpu.SemaphoreType.DMA
+    stacked = small_call(
+        stack_kernel, rest.shape, [pl.ANY, pl.ANY], "stack_rows", flops=LONG,
+        input_output_aliases={0: 0},
+        scratch_shapes=[vmem(single.shape, single.dtype), dma((4,)), dma((4,))],
+    )(pair, single)
     rest = lax.all_to_all(rest, "seq", split_axis=0, concat_axis=0, tiled=True)
     half = (2 * TILE, H * HD)
-    done = small_call(place_rows, half, [smem, vmem], "place_rows",1000)(slots, rest)
+    place_scratch = [vmem(rest.shape, rest.dtype), vmem(half, rest.dtype), dma((4,)), dma((4,))]
+    done = small_call(
+        place_kernel, half, [smem, pl.ANY], "place_rows", scratch_shapes=place_scratch
+    )(slots, rest)
     stacked = small_call(
-        after_kernel, rest.shape, [pl.ANY, pl.ANY], "rows_after", 1000, pl.ANY,
-        input_output_aliases={0: 0},
+        after_kernel, rest.shape, [pl.ANY, pl.ANY], "rows_after", input_output_aliases={0: 0}
     )(stacked, done)
     done = next_section(done, range(owners))
-    whole = (2 * half[0], half[1])
-    dma = pltpu.SemaphoreType.DMA
-    laid = small_call(
-        lay_kernel, whole, [vmem], "lay_rows", LONG, pl.ANY, scratch_shapes=[dma]
+    done = small_call(
+        same_kernel, half, [pl.ANY], "rows_shifted", flops=LONG, input_output_aliases={0: 0}
     )(done)
     moved = lax.all_to_all(stacked, "seq", split_axis=0, concat_axis=0, tiled=True)
     return small_call(
-        join_kernel, whole, [smem, vmem, pl.ANY], "join_rows", kind=pl.ANY,
-        input_output_aliases={2: 0}, scratch_shapes=[vmem(half, jnp.bfloat16), dma],
-    )(slots, moved, laid)[None]
+        join_kernel, (2 * half[0], half[1]), [smem, pl.ANY, pl.ANY], "join_rows",
+        scratch_shapes=place_scratch + [vmem(half, rest.dtype), dma((2, 4))],
+    )(slots, moved, done)[None]
 
 
 def solution(mesh):

time: 264 us -> 265 us (level)
  Pallas kernels: 43.1 us -> 40.4 us
  transfers between devices with their start and end apart: 5 -> 5, of which waited for: 2 -> 2; matrix products, arithmetic and copies ran while one was open for 0% -> 0% of each run, Pallas kernels for 3% -> 2%
where the time goes in v5:
time: 265 us; the launch traced here: 263 us
  blocking collectives  149 us (56%)
  waiting for transfers between devices  52.8 us (20%)
  Pallas kernels  40.4 us (15%)
  starting transfers between devices  19.4 us (7%)
    all_to_all x1, blocking collectives, local(): lax.all_to_all(packed, 'seq', split_axis=0, concat_axis=0, tiled=True)  149 us
    ppermute x3, waiting for transfers between devices, next_section(): return lax.ppermute(block, ('section', 'seq'), route)  28.1 us
    all_to_all x1, waiting for transfers between devices, local(): rest = lax.all_to_all(rest, 'seq', split_axis=0, concat_axis=0, tiled=True)  24.7 us
    pallas_call x1, Pallas kernels, attend(): pl.pallas_call(attend_kernel, out_shape=(pair, part, jax.ShapeDtypeStruct...  20 us
    pallas_call x1, Pallas kernels, pack(): pl.pallas_call(pack_kernel, out_shape=(jax.ShapeDtypeStruct((SLOTS, 3, x....  10.1 us
    all_to_all x1, starting transfers between devices, local(): rest = lax.all_to_all(rest, 'seq', split_axis=0, concat_axis=0, tiled=True)  7.6 us
    ppermute x3, starting transfers between devices, next_section(): return lax.ppermute(block, ('section', 'seq'), route)  7.27 us
  transfers between devices with their start and end apart: 5, of which 2 were waited for; matrix products, arithmetic and copies ran while one was open for 0% of the time, Pallas kernels for 2%

profile of v5, /device:TPU:1, one launch (start us, length us, event | category | flops | bytes accessed | tf_op | source)
XLA Modules:
  0.0 263.2 jit_solution(17471599533715247208)
XLA Ops:
  0.0 10.1 %pack_heads.1 = (bf16[32,3,512,128]{3,2,1,0:T(8,128)(2,1)}, s32[40]{0:T(128)}) custom-call(s32[24,128]{1,0:T(8,128)} %counts_ref.3, bf16[3,512,3072]{2,1,0:T(8,128)(2,1)} %bitcast.7), custom_call_target="tpu_custom_call" | custom-call | bytes 25000000 | tf_op jit(solution)/shard_map/pack_heads/pallas_call | solution.py:65
  10.1 149.2 %all_to_all.15 = bf16[32,3,512,128]{3,2,1,0:T(8,128)(2,1)} all-to-all(bf16[32,3,512,128]{3,2,1,0:T(8,128)(2,1)} %get-tuple-element.11), channel_id=1, replica_groups=mesh['section'=4,'seq'=32] {'seq'}, dimensions={0} | all-to-all | bytes 25165824 | tf_op jit(solution)/shard_map/all_to_all | solution.py:344
  159.3 20.0 %attend_tiles.1 = (bf16[32,2,128,128]{3,2,1,0:T(8,128)(2,1)}, bf16[32,128,128]{2,1,0:T(8,128)(2,1)}, bf16[32,2,128,128]{3,2,1,0:T(8,128)(2,1)}) custom-call(s32[40]{0:T(128)} %get-tuple-element.10.slot_ref, s32[24]{0:T(128)} %class_ref.1, s32[16,128]{1,0:T(8,128)} %bitcast.8, s32[24,128]{1,0:T(8,128)} %counts_ref.3, bf16[1,3072]{1,0:T(2,128)(2,1)} %gate_ref.1, ...), custom_call_target="tpu_custom_call" | custom-call | flops 20000000000 | bytes 17000000 | tf_op jit(solution)/shard_map/attend_tiles/pallas_call | solution.py:208
  179.2 2.0 collective-permute-start
  181.3 0.0 copy-start.1
  181.3 7.6 %all-to-all-start.1 = ((bf16[32,2,128,128]{3,2,1,0:T(8,128)(2,1)}), bf16[32,2,128,128]{3,2,1,0:T(8,128)(2,1)S(1)}, u32[]{:S(2)}, u32[]{:S(2)}) async-start(bf16[32,2,128,128]{3,2,1,0:T(8,128)(2,1)} %get-tuple-element.14), calls=%async_computation.1 | async-start | bytes 4194304 | tf_op jit(solution)/shard_map/all_to_all | solution.py:356
  188.9 0.0 copy-done.1
  188.9 3.6 %collective-permute-start.1 = (bf16[32,128,128]{2,1,0:T(8,128)(2,1)S(1)}, bf16[32,128,128]{2,1,0:T(8,128)(2,1)}, u32[]{:S(2)}, u32[]{:S(2)}) collective-permute-start(bf16[32,128,128]{2,1,0:T(8,128)(2,1)S(1)} %copy-done.1), channel_id=1, source_target_pairs={{1,33},{3,35},{5,37},{7,39},{9,41},{11,43},{13,45},{15,47},{17,49}... | collective-permute-start | bytes 3145736 | tf_op jit(solution)/shard_map/ppermute | solution.py:338
  192.4 24.7 %all-to-all-done.1.rows_ref = bf16[32,2,128,128]{3,2,1,0:T(8,128)(2,1)S(1)} async-done(((bf16[32,2,128,128]{3,2,1,0:T(8,128)(2,1)}), bf16[32,2,128,128]{3,2,1,0:T(8,128)(2,1)S(1)}, u32[]{:S(2)}, u32[]{:S(2)}) %all-to-all-start.1) | async-done | bytes 2097184 | tf_op jit(solution)/shard_map/all_to_all | solution.py:356
  217.2 0.0 copy-start
  217.2 1.3 copy-done
  218.5 3.5 %place_rows.1.before_ref = bf16[256,3072]{1,0:T(8,128)(2,1)} custom-call(s32[40]{0:T(128)} %get-tuple-element.10.slot_ref, bf16[32,2,128,128]{3,2,1,0:T(8,128)(2,1)} %copy-done), custom_call_target="tpu_custom_call" | custom-call | bytes 1000 | tf_op jit(solution)/shard_map/place_rows/pallas_call | solution.py:359
  222.0 1.7 collective-permute-start.2
  223.7 0.0 collective-permute-done.1.single_ref
  223.7 0.0 collective-permute-done.pair_ref
  223.7 2.3 stack_rows.1.in_ref
  226.0 4.6 %all-to-all-start.2 = ((bf16[32,2,128,128]{3,2,1,0:T(8,128)(2,1)}), bf16[32,2,128,128]{3,2,1,0:T(8,128)(2,1)}, u32[]{:S(2)}, u32[]{:S(2)}) async-start(bf16[32,2,128,128]{3,2,1,0:T(8,128)(2,1)} %rows_after.1), calls=%async_computation.2 | async-start | bytes 4194304 | tf_op jit(solution)/shard_map/all_to_all | solution.py:369
  230.6 28.1 %collective-permute-done.2.in_ref = bf16[256,3072]{1,0:T(8,128)(2,1)} collective-permute-done((bf16[256,3072]{1,0:T(8,128)(2,1)}, bf16[256,3072]{1,0:T(8,128)(2,1)}, u32[]{:S(2)}, u32[]{:S(2)}) %collective-permute-start.2) | collective-permute-done | bytes 1572896 | tf_op jit(solution)/shard_map/ppermute | solution.py:338
  258.7 0.0 all-to-all-done.2.rows_ref
  258.7 4.6 %join_rows.1 = bf16[512,3072]{1,0:T(8,128)(2,1)} custom-call(s32[40]{0:T(128)} %get-tuple-element.10.slot_ref, bf16[32,2,128,128]{3,2,1,0:T(8,128)(2,1)} %all-to-all-done.2.rows_ref, bf16[256,3072]{1,0:T(8,128)(2,1)} %rows_shifted.1.done_ref), custom_call_target="tpu_custom_call" | custom-call | bytes 1000 | tf_op jit(solution)/shard_map/join_rows/pallas_call | solution.py:370
  (2 shorter events, 0.0 us)
Async XLA Ops:
  179.2 44.5 %collective-permute-start = (bf16[32,2,128,128]{3,2,1,0:T(8,128)(2,1)}, bf16[32,2,128,128]{3,2,1,0:T(8,128)(2,1)}, u32[]{:S(2)}, u32[]{:S(2)}) collective-permute-start(bf16[32,2,128,128]{3,2,1,0:T(8,128)(2,1)} %get-tuple-element.12), channel_id=1, source_target_pairs={{0,32},{2,34},{4,36},{6,38},{8,40},{10,42},{12,44},{14,46},{16,48}... | collective-permute-start | bytes 6291464 | tf_op jit(solution)/shard_map/ppermute | solution.py:338
  181.3 7.6 %copy-start.1 = (bf16[32,128,128]{2,1,0:T(8,128)(2,1)S(1)}, bf16[32,128,128]{2,1,0:T(8,128)(2,1)}, u32[]{:S(2)}) copy-start(bf16[32,128,128]{2,1,0:T(8,128)(2,1)} %get-tuple-element.13) | copy-start | bytes 3145732
  181.3 35.9 %all-to-all-start.1 = ((bf16[32,2,128,128]{3,2,1,0:T(8,128)(2,1)}), bf16[32,2,128,128]{3,2,1,0:T(8,128)(2,1)S(1)}, u32[]{:S(2)}, u32[]{:S(2)}) async-start(bf16[32,2,128,128]{3,2,1,0:T(8,128)(2,1)} %get-tuple-element.14), calls=%async_computation.1 | async-start | bytes 4194304 | tf_op jit(solution)/shard_map/all_to_all | solution.py:356
  188.9 34.9 %collective-permute-start.1 = (bf16[32,128,128]{2,1,0:T(8,128)(2,1)S(1)}, bf16[32,128,128]{2,1,0:T(8,128)(2,1)}, u32[]{:S(2)}, u32[]{:S(2)}) collective-permute-start(bf16[32,128,128]{2,1,0:T(8,128)(2,1)S(1)} %copy-done.1), channel_id=1, source_target_pairs={{1,33},{3,35},{5,37},{7,39},{9,41},{11,43},{13,45},{15,47},{17,49}... | collective-permute-start | bytes 3145736 | tf_op jit(solution)/shard_map/ppermute | solution.py:338
  217.2 1.3 copy-start
  222.0 36.6 %collective-permute-start.2 = (bf16[256,3072]{1,0:T(8,128)(2,1)}, bf16[256,3072]{1,0:T(8,128)(2,1)}, u32[]{:S(2)}, u32[]{:S(2)}) collective-permute-start(bf16[256,3072]{1,0:T(8,128)(2,1)} %place_rows.1.before_ref), channel_id=1, source_target_pairs={{0,32},{1,33},{2,34},{3,35},{4,36},{5,37},{6,38},{7,39},{8,40},{9,... | collective-permute-start | bytes 4718600 | tf_op jit(solution)/shard_map/ppermute | solution.py:338
  226.0 32.6 %all-to-all-start.2 = ((bf16[32,2,128,128]{3,2,1,0:T(8,128)(2,1)}), bf16[32,2,128,128]{3,2,1,0:T(8,128)(2,1)}, u32[]{:S(2)}, u32[]{:S(2)}) async-start(bf16[32,2,128,128]{3,2,1,0:T(8,128)(2,1)} %rows_after.1), calls=%async_computation.2 | async-start | bytes 4194304 | tf_op jit(solution)/shard_map/all_to_all | solution.py:369

commit v6 on v5

--- a/solution.py
+++ b/solution.py
@@ -85,19 +85,9 @@
 def attend_kernel(
     slot_ref, class_ref, lists_ref, counts_ref, gate_ref, x_ref,
     pair_ref, single_ref, rest_ref,
-    held, result, sorted_ref, start_ref, in_sems, out_sems,
+    result, sorted_ref, start_ref, out_sems,
 ):
-    pieces = in_sems.shape[0]
     owners = x_ref.shape[0]
-    width = x_ref.shape[0] // pieces
-    loads = [
-        pltpu.make_async_copy(
-            x_ref.at[pl.ds(i * width, width)], held.at[pl.ds(i * width, width)], in_sems.at[i]
-        )
-        for i in range(pieces)
-    ]
-    for load in loads:
-        load.start()
 
     me = lax.axis_index("seq")
     shared = lax.rem(me, 2)
@@ -134,11 +124,9 @@
     lax.fori_loop(0, total // 8, lambda i, carry: [place(8 * i + u, 0) for u in range(8)][-1], 0)
     gate = gate_ref[:, pl.ds(pl.multiple_of(head * HD, HD), HD)].astype(jnp.float32)
     ones = jnp.ones((TILE, HD), jnp.bfloat16)
-    for load in loads:
-        load.wait()
 
     def tile_of(which, t):
-        return held[t // 4, which, lax.rem(t, 4)]
+        return x_ref[t // 4, which, lax.rem(t, 4)]
 
     for c in range(1, KMAX + 1):
         group = max(1, PAIRS // c)
@@ -202,23 +190,22 @@
 def attend(slots, head_class, lists, counts, gate, arrived):
     owners = arrived.shape[0]
     smem = pl.BlockSpec(memory_space=pltpu.SMEM)
+    vmem = pl.BlockSpec(memory_space=pltpu.VMEM)
     anywhere = pl.BlockSpec(memory_space=pl.ANY)
     part = jax.ShapeDtypeStruct((owners, TILE, HD), jnp.bfloat16)
     pair = jax.ShapeDtypeStruct((owners, 2, TILE, HD), jnp.bfloat16)
     return pl.pallas_call(
         attend_kernel,
         out_shape=(pair, part, jax.ShapeDtypeStruct((owners, 2, TILE, HD), jnp.bfloat16)),
-        in_specs=[smem, smem, smem, smem, pl.BlockSpec(memory_space=pltpu.VMEM), anywhere],
+        in_specs=[smem, smem, smem, smem, vmem, vmem],
         out_specs=(anywhere, anywhere, anywhere),
         scratch_shapes=[
-            pltpu.VMEM(arrived.shape, jnp.bfloat16),
             pltpu.VMEM((4, owners, TILE, HD), jnp.bfloat16),
             pltpu.SMEM((owners * 4,), jnp.int32),
             pltpu.SMEM((KMAX + 2,), jnp.int32),
-            pltpu.SemaphoreType.DMA((8,)),
             pltpu.SemaphoreType.DMA((5,)),
         ],
-        compiler_params=pltpu.CompilerParams(vmem_limit_bytes=60 * 1024 * 1024),
+        compiler_params=pltpu.CompilerParams(vmem_limit_bytes=20 * 1024 * 1024),
         cost_estimate=pl.CostEstimate(
             flops=20_000_000_000, bytes_accessed=17_000_000, transcendentals=8_000_000
         ),

time: 265 us -> 259 us (0.977)
  Pallas kernels: 40.4 us -> 36.7 us
    pallas_call x1, Pallas kernels: 20 us -> 16.4 us  [attend(): pl.pallas_call(attend_kernel, out_shape=(pair, part, jax.ShapeDtypeStruct...]
where the time goes in v6:
time: 259 us; the launch traced here: 258 us
  blocking collectives  149 us (58%)
  waiting for transfers between devices  52.9 us (20%)
  Pallas kernels  36.7 us (14%)
  starting transfers between devices  19.3 us (7%)
    all_to_all x1, blocking collectives, local(): lax.all_to_all(packed, 'seq', split_axis=0, concat_axis=0, tiled=True)  149 us
    ppermute x3, waiting for transfers between devices, next_section(): return lax.ppermute(block, ('section', 'seq'), route)  28.1 us
    all_to_all x1, waiting for transfers between devices, local(): rest = lax.all_to_all(rest, 'seq', split_axis=0, concat_axis=0, tiled=True)  24.8 us
    pallas_call x1, Pallas kernels, attend(): pl.pallas_call(attend_kernel, out_shape=(pair, part, jax.ShapeDtypeStruct...  16.4 us
    pallas_call x1, Pallas kernels, pack(): pl.pallas_call(pack_kernel, out_shape=(jax.ShapeDtypeStruct((SLOTS, 3, x....  9.99 us
    all_to_all x1, starting transfers between devices, local(): rest = lax.all_to_all(rest, 'seq', split_axis=0, concat_axis=0, tiled=True)  7.54 us
    ppermute x3, starting transfers between devices, next_section(): return lax.ppermute(block, ('section', 'seq'), route)  7.24 us
  transfers between devices with their start and end apart: 5, of which 2 were waited for; matrix products, arithmetic and copies ran while one was open for 0% of the time, Pallas kernels for 2%

profile of v6, /device:TPU:1, one launch (start us, length us, event | category | flops | bytes accessed | tf_op | source)
XLA Modules:
  0.0 258.3 jit_solution(2887429213990871497)
XLA Ops:
  0.0 10.0 %pack_heads.1 = (bf16[32,3,512,128]{3,2,1,0:T(8,128)(2,1)}, s32[40]{0:T(128)}) custom-call(s32[24,128]{1,0:T(8,128)} %counts_ref.3, bf16[3,512,3072]{2,1,0:T(8,128)(2,1)} %bitcast.8), custom_call_target="tpu_custom_call" | custom-call | bytes 25000000 | tf_op jit(solution)/shard_map/pack_heads/pallas_call | solution.py:65
  10.0 0.0 copy-start
  10.0 0.0 copy-start.1
  10.0 0.0 copy-start.2
  10.0 0.0 copy-start.3
  10.0 0.0 copy-start.4
  10.1 149.2 %all_to_all.15 = bf16[32,3,512,128]{3,2,1,0:T(8,128)(2,1)S(1)} all-to-all(bf16[32,3,512,128]{3,2,1,0:T(8,128)(2,1)} %get-tuple-element.11), channel_id=1, replica_groups=mesh['section'=4,'seq'=32] {'seq'}, dimensions={0} | all-to-all | bytes 25165824 | tf_op jit(solution)/shard_map/all_to_all | solution.py:331
  159.3 0.0 copy-done
  159.3 0.0 copy-done.1
  159.3 0.0 copy-done.2
  159.3 16.4 %attend_tiles.1 = (bf16[32,2,128,128]{3,2,1,0:T(8,128)(2,1)S(1)}, bf16[32,128,128]{2,1,0:T(8,128)(2,1)S(1)}, bf16[32,2,128,128]{3,2,1,0:T(8,128)(2,1)}) custom-call(s32[40]{0:T(128)S(1)} %copy-done.1, s32[24]{0:T(128)S(1)} %copy-done.4, s32[16,128]{1,0:T(8,128)S(1)} %bitcast.7, s32[24,128]{1,0:T(8,128)S(1)} %copy-done, bf16[1,3072]{1,0:T(2,128)(2,1)S(1)} %copy-done.2, ...), custom_call_target="tpu_custom_call" | custom-call | flops 20000000000 | bytes 17000000 | tf_op jit(solution)/shard_map/attend_tiles/pallas_call | solution.py:197
  175.7 2.0 collective-permute-start
  177.7 7.5 %all-to-all-start.1 = ((bf16[32,2,128,128]{3,2,1,0:T(8,128)(2,1)}), bf16[32,2,128,128]{3,2,1,0:T(8,128)(2,1)}, u32[]{:S(2)}, u32[]{:S(2)}) async-start(bf16[32,2,128,128]{3,2,1,0:T(8,128)(2,1)} %get-tuple-element.14), calls=%async_computation.1 | async-start | bytes 4194304 | tf_op jit(solution)/shard_map/all_to_all | solution.py:343
  185.3 3.5 %collective-permute-start.1 = (bf16[32,128,128]{2,1,0:T(8,128)(2,1)S(1)}, bf16[32,128,128]{2,1,0:T(8,128)(2,1)}, u32[]{:S(2)}, u32[]{:S(2)}) collective-permute-start(bf16[32,128,128]{2,1,0:T(8,128)(2,1)S(1)} %get-tuple-element.13), channel_id=1, source_target_pairs={{1,33},{3,35},{5,37},{7,39},{9,41},{11,43},{13,45},{15,47},{17,49}... | collective-permute-start | bytes 3145736 | tf_op jit(solution)/shard_map/ppermute | solution.py:325
  188.8 24.8 %all-to-all-done.1.rows_ref = bf16[32,2,128,128]{3,2,1,0:T(8,128)(2,1)} async-done(((bf16[32,2,128,128]{3,2,1,0:T(8,128)(2,1)}), bf16[32,2,128,128]{3,2,1,0:T(8,128)(2,1)}, u32[]{:S(2)}, u32[]{:S(2)}) %all-to-all-start.1) | async-done | bytes 2097184 | tf_op jit(solution)/shard_map/all_to_all | solution.py:343
  213.6 3.5 %place_rows.1.before_ref = bf16[256,3072]{1,0:T(8,128)(2,1)} custom-call(s32[40]{0:T(128)} %get-tuple-element.10.slot_ref, bf16[32,2,128,128]{3,2,1,0:T(8,128)(2,1)} %all-to-all-done.1.rows_ref), custom_call_target="tpu_custom_call" | custom-call | bytes 1000 | tf_op jit(solution)/shard_map/place_rows/pallas_call | solution.py:346
  217.1 1.7 collective-permute-start.2
  218.8 0.0 collective-permute-done.1.single_ref
  218.8 0.0 collective-permute-done.pair_ref
  218.8 2.3 stack_rows.1.in_ref
  221.1 4.6 %all-to-all-start.2 = ((bf16[32,2,128,128]{3,2,1,0:T(8,128)(2,1)}), bf16[32,2,128,128]{3,2,1,0:T(8,128)(2,1)}, u32[]{:S(2)}, u32[]{:S(2)}) async-start(bf16[32,2,128,128]{3,2,1,0:T(8,128)(2,1)} %rows_after.1), calls=%async_computation.2 | async-start | bytes 4194304 | tf_op jit(solution)/shard_map/all_to_all | solution.py:356
  225.7 28.1 %collective-permute-done.2.in_ref = bf16[256,3072]{1,0:T(8,128)(2,1)} collective-permute-done((bf16[256,3072]{1,0:T(8,128)(2,1)}, bf16[256,3072]{1,0:T(8,128)(2,1)}, u32[]{:S(2)}, u32[]{:S(2)}) %collective-permute-start.2) | collective-permute-done | bytes 1572896 | tf_op jit(solution)/shard_map/ppermute | solution.py:325
  253.8 0.0 all-to-all-done.2.rows_ref
  253.8 4.6 %join_rows.1 = bf16[512,3072]{1,0:T(8,128)(2,1)} custom-call(s32[40]{0:T(128)} %get-tuple-element.10.slot_ref, bf16[32,2,128,128]{3,2,1,0:T(8,128)(2,1)} %all-to-all-done.2.rows_ref, bf16[256,3072]{1,0:T(8,128)(2,1)} %rows_shifted.1.done_ref), custom_call_target="tpu_custom_call" | custom-call | bytes 1000 | tf_op jit(solution)/shard_map/join_rows/pallas_call | solution.py:357
  (4 shorter events, 0.0 us)
Async XLA Ops:
  10.0 149.3 %copy-start = (s32[24,128]{1,0:T(8,128)S(1)}, s32[24,128]{1,0:T(8,128)}, u32[]{:S(2)}) copy-start(s32[24,128]{1,0:T(8,128)} %counts_ref.3) | copy-start | bytes 36868
  10.0 149.3 %copy-start.1 = (s32[40]{0:T(128)S(1)}, s32[40]{0:T(128)}, u32[]{:S(2)}) copy-start(s32[40]{0:T(128)} %get-tuple-element.10.slot_ref) | copy-start | bytes 484
  10.0 149.3 %copy-start.2 = (bf16[1,3072]{1,0:T(2,128)(2,1)S(1)}, bf16[1,3072]{1,0:T(2,128)(2,1)}, u32[]{:S(2)}) copy-start(bf16[1,3072]{1,0:T(2,128)(2,1)} %gate_ref.1) | copy-start | bytes 18436
  10.0 149.3 %copy-start.3 = (s32[2,128,8]{1,2,0:T(8,128)S(1)}, s32[2,128,8]{1,2,0:T(8,128)}, u32[]{:S(2)}) copy-start(s32[2,128,8]{1,2,0:T(8,128)} %param.8) | copy-start | bytes 24580
  10.0 149.3 %copy-start.4 = (s32[24]{0:T(128)S(1)}, s32[24]{0:T(128)}, u32[]{:S(2)}) copy-start(s32[24]{0:T(128)} %class_ref.1) | copy-start | bytes 292
  175.7 43.1 %collective-permute-start = (bf16[32,2,128,128]{3,2,1,0:T(8,128)(2,1)S(1)}, bf16[32,2,128,128]{3,2,1,0:T(8,128)(2,1)}, u32[]{:S(2)}, u32[]{:S(2)}) collective-permute-start(bf16[32,2,128,128]{3,2,1,0:T(8,128)(2,1)S(1)} %get-tuple-element.12), channel_id=1, source_target_pairs={{0,32},{2,34},{4,36},{6,38},{8,40},{10,42},{12,44},{14,46},{16,48}... | collective-permute-start | bytes 6291464 | tf_op jit(solution)/shard_map/ppermute | solution.py:325
  177.7 35.9 %all-to-all-start.1 = ((bf16[32,2,128,128]{3,2,1,0:T(8,128)(2,1)}), bf16[32,2,128,128]{3,2,1,0:T(8,128)(2,1)}, u32[]{:S(2)}, u32[]{:S(2)}) async-start(bf16[32,2,128,128]{3,2,1,0:T(8,128)(2,1)} %get-tuple-element.14), calls=%async_computation.1 | async-start | bytes 4194304 | tf_op jit(solution)/shard_map/all_to_all | solution.py:343
  185.3 33.6 %collective-permute-start.1 = (bf16[32,128,128]{2,1,0:T(8,128)(2,1)S(1)}, bf16[32,128,128]{2,1,0:T(8,128)(2,1)}, u32[]{:S(2)}, u32[]{:S(2)}) collective-permute-start(bf16[32,128,128]{2,1,0:T(8,128)(2,1)S(1)} %get-tuple-element.13), channel_id=1, source_target_pairs={{1,33},{3,35},{5,37},{7,39},{9,41},{11,43},{13,45},{15,47},{17,49}... | collective-permute-start | bytes 3145736 | tf_op jit(solution)/shard_map/ppermute | solution.py:325
  217.1 36.6 %collective-permute-start.2 = (bf16[256,3072]{1,0:T(8,128)(2,1)}, bf16[256,3072]{1,0:T(8,128)(2,1)}, u32[]{:S(2)}, u32[]{:S(2)}) collective-permute-start(bf16[256,3072]{1,0:T(8,128)(2,1)} %place_rows.1.before_ref), channel_id=1, source_target_pairs={{0,32},{1,33},{2,34},{3,35},{4,36},{5,37},{6,38},{7,39},{8,40},{9,... | collective-permute-start | bytes 4718600 | tf_op jit(solution)/shard_map/ppermute | solution.py:325
  221.1 32.7 %all-to-all-start.2 = ((bf16[32,2,128,128]{3,2,1,0:T(8,128)(2,1)}), bf16[32,2,128,128]{3,2,1,0:T(8,128)(2,1)}, u32[]{:S(2)}, u32[]{:S(2)}) async-start(bf16[32,2,128,128]{3,2,1,0:T(8,128)(2,1)} %rows_after.1), calls=%async_computation.2 | async-start | bytes 4194304 | tf_op jit(solution)/shard_map/all_to_all | solution.py:356

commit v7 on v6

--- a/solution.py
+++ b/solution.py
@@ -213,32 +213,17 @@
     )(slots, head_class, lists, counts, gate, arrived)
 
 
-def place_rows(slot_ref, rows_ref, out_ref, held, half, in_sems, out_sems):
-    pieces = in_sems.shape[0]
-    width, chips = rows_ref.shape[0] // pieces, CHIPS // pieces
-    loads = [
-        pltpu.make_async_copy(
-            rows_ref.at[pl.ds(n * width, width)], held.at[pl.ds(n * width, width)], in_sems.at[n]
-        )
-        for n in range(pieces)
-    ]
-    for load in loads:
-        load.start()
-    for n in range(pieces):
-        loads[n].wait()
-
-        def one_chip(i, carry, n=n):
-            chip = n * chips + i
-            columns = pl.ds(pl.multiple_of(slot_ref[2 * chip] * HD, HD), HD)
-            half[:TILE, columns] = held[2 * chip, 0]
-            half[TILE:, columns] = held[2 * chip, 1]
-            columns = pl.ds(pl.multiple_of(slot_ref[2 * chip + 1] * HD, HD), HD)
-            start = pl.multiple_of(chip // SHARED * TILE, TILE)
-            half[pl.ds(start, TILE), columns] = held[2 * chip + 1, 0]
-            return carry
-
-        lax.fori_loop(0, chips, one_chip, 0)
-    return send_rows(half, out_ref, out_sems)
+def place_rows(slot_ref, rows_ref, out_ref):
+    def one_chip(chip, carry):
+        columns = pl.ds(pl.multiple_of(slot_ref[2 * chip] * HD, HD), HD)
+        out_ref[:TILE, columns] = rows_ref[2 * chip, 0]
+        out_ref[TILE:, columns] = rows_ref[2 * chip, 1]
+        columns = pl.ds(pl.multiple_of(slot_ref[2 * chip + 1] * HD, HD), HD)
+        start = pl.multiple_of(chip // SHARED * TILE, TILE)
+        out_ref[pl.ds(start, TILE), columns] = rows_ref[2 * chip + 1, 0]
+        return carry
+
+    lax.fori_loop(0, CHIPS, one_chip, 0)
 
 
 def send_rows(source, target, sems):
@@ -255,20 +240,11 @@
     return copies
 
 
-def place_kernel(slot_ref, rows_ref, out_ref, held, half, in_sems, out_sems):
-    for copy in place_rows(slot_ref, rows_ref, out_ref, held, half, in_sems, out_sems):
-        copy.wait()
-
-
-def join_kernel(
-    slot_ref, rows_ref, done_ref, out_ref, held, half, in_sems, out_sems, other, other_sems
-):
-    arrivals = send_rows(done_ref, other, other_sems.at[0])
+def join_kernel(slot_ref, rows_ref, done_ref, out_ref, half, sems):
     rows = half.shape[0]
-    copies = place_rows(slot_ref, rows_ref, out_ref, held, half, in_sems, out_sems)
-    for arrival in arrivals:
-        arrival.wait()
-    copies += send_rows(other, out_ref.at[pl.ds(rows, rows)], other_sems.at[1])
+    copies = send_rows(done_ref, out_ref.at[pl.ds(rows, rows)], sems.at[0])
+    place_rows(slot_ref, rows_ref, half)
+    copies += send_rows(half, out_ref.at[pl.ds(0, rows)], sems.at[1])
     for copy in copies:
         copy.wait()
 
@@ -307,7 +283,7 @@
         out_shape=jax.ShapeDtypeStruct(shape, jnp.bfloat16),
         in_specs=[pl.BlockSpec(memory_space=k) for k in kinds],
         out_specs=pl.BlockSpec(memory_space=kind),
-        compiler_params=pltpu.CompilerParams(vmem_limit_bytes=60 * 1024 * 1024),
+        compiler_params=pltpu.CompilerParams(vmem_limit_bytes=16 * 1024 * 1024),
         cost_estimate=pl.CostEstimate(flops=flops, bytes_accessed=1000, transcendentals=0),
         name=name,
         **more,
@@ -342,10 +318,7 @@
     )(pair, single)
     rest = lax.all_to_all(rest, "seq", split_axis=0, concat_axis=0, tiled=True)
     half = (2 * TILE, H * HD)
-    place_scratch = [vmem(rest.shape, rest.dtype), vmem(half, rest.dtype), dma((4,)), dma((4,))]
-    done = small_call(
-        place_kernel, half, [smem, pl.ANY], "place_rows", scratch_shapes=place_scratch
-    )(slots, rest)
+    done = small_call(place_rows, half, [smem, vmem], "place_rows", vmem)(slots, rest)
     stacked = small_call(
         after_kernel, rest.shape, [pl.ANY, pl.ANY], "rows_after", input_output_aliases={0: 0}
     )(stacked, done)
@@ -355,8 +328,8 @@
     )(done)
     moved = lax.all_to_all(stacked, "seq", split_axis=0, concat_axis=0, tiled=True)
     return small_call(
-        join_kernel, (2 * half[0], half[1]), [smem, pl.ANY, pl.ANY], "join_rows",
-        scratch_shapes=place_scratch + [vmem(half, rest.dtype), dma((2, 4))],
+        join_kernel, (2 * half[0], half[1]), [smem, vmem, vmem], "join_rows",
+        scratch_shapes=[vmem(half, rest.dtype), dma((2, 4))],
     )(slots, moved, done)[None]
 
 

time: 259 us -> 258 us (level)
  Pallas kernels: 36.7 us -> 32 us
  starting transfers between devices: 19.3 us -> 22.4 us
    all_to_all x1, starting transfers between devices: 7.54 us -> 10.7 us  [local(): rest = lax.all_to_all(rest, 'seq', split_axis=0, concat_axis=0, tiled=True)]
    pallas_call x1, Pallas kernels: 16.4 us -> 13.8 us  [attend(): pl.pallas_call(attend_kernel, out_shape=(pair, part, jax.ShapeDtypeStruct...]
where the time goes in v7:
time: 258 us
  blocking collectives  149 us (58%)
  waiting for transfers between devices  52.8 us (20%)
  Pallas kernels  32 us (12%)
  starting transfers between devices  22.4 us (9%)
    all_to_all x1, blocking collectives, local(): lax.all_to_all(packed, 'seq', split_axis=0, concat_axis=0, tiled=True)  149 us
    ppermute x3, waiting for transfers between devices, next_section(): return lax.ppermute(block, ('section', 'seq'), route)  28.1 us
    all_to_all x1, waiting for transfers between devices, local(): rest = lax.all_to_all(rest, 'seq', split_axis=0, concat_axis=0, tiled=True)  24.7 us
    pallas_call x1, Pallas kernels, attend(): pl.pallas_call(attend_kernel, out_shape=(pair, part, jax.ShapeDtypeStruct...  13.8 us
    all_to_all x1, starting transfers between devices, local(): rest = lax.all_to_all(rest, 'seq', split_axis=0, concat_axis=0, tiled=True)  10.7 us
    pallas_call x1, Pallas kernels, pack(): pl.pallas_call(pack_kernel, out_shape=(jax.ShapeDtypeStruct((SLOTS, 3, x....  10 us
    ppermute x3, starting transfers between devices, next_section(): return lax.ppermute(block, ('section', 'seq'), route)  7.17 us
  transfers between devices with their start and end apart: 5, of which 2 were waited for; matrix products, arithmetic and copies ran while one was open for 0% of the time, Pallas kernels for 2%

profile of v7, /device:TPU:1, one launch (start us, length us, event | category | flops | bytes accessed | tf_op | source)
XLA Modules:
  0.0 258.0 jit_solution(7681003004047785290)
XLA Ops:
  0.0 10.0 %pack_heads.1 = (bf16[32,3,512,128]{3,2,1,0:T(8,128)(2,1)}, s32[40]{0:T(128)}) custom-call(s32[24,128]{1,0:T(8,128)} %counts_ref.3, bf16[3,512,3072]{2,1,0:T(8,128)(2,1)} %bitcast.8), custom_call_target="tpu_custom_call" | custom-call | bytes 25000000 | tf_op jit(solution)/shard_map/pack_heads/pallas_call | solution.py:65
  10.0 0.0 copy-start.1
  10.0 0.0 copy-start.2
  10.1 0.0 copy-start.3
  10.1 0.0 copy-start.4
  10.1 0.0 copy-start.5
  10.1 149.2 %all_to_all.15 = bf16[32,3,512,128]{3,2,1,0:T(8,128)(2,1)S(1)} all-to-all(bf16[32,3,512,128]{3,2,1,0:T(8,128)(2,1)} %get-tuple-element.11), channel_id=1, replica_groups=mesh['section'=4,'seq'=32] {'seq'}, dimensions={0} | all-to-all | bytes 25165824 | tf_op jit(solution)/shard_map/all_to_all | solution.py:307
  159.3 0.0 copy-done.1
  159.3 0.0 copy-done.2
  159.4 13.8 %attend_tiles.1 = (bf16[32,2,128,128]{3,2,1,0:T(8,128)(2,1)}, bf16[32,128,128]{2,1,0:T(8,128)(2,1)S(1)}, bf16[32,2,128,128]{3,2,1,0:T(8,128)(2,1)S(1)}) custom-call(s32[40]{0:T(128)S(1)} %copy-done.2, s32[24]{0:T(128)S(1)} %copy-done.5, s32[16,128]{1,0:T(8,128)S(1)} %bitcast.7, s32[24,128]{1,0:T(8,128)S(1)} %copy-done.1, bf16[1,3072]{1,0:T(2,128)(2,1)S(1)} %copy-done.3, ...), custom_call_target="tpu_custom_call" | custom-call | flops 20000000000 | bytes 17000000 | tf_op jit(solution)/shard_map/attend_tiles/pallas_call | solution.py:197
  173.2 1.3 copy-done
  174.5 2.0 collective-permute-start
  176.5 10.7 %all-to-all-start.1 = ((bf16[32,2,128,128]{3,2,1,0:T(8,128)(2,1)}), bf16[32,2,128,128]{3,2,1,0:T(8,128)(2,1)S(1)}, u32[]{:S(2)}, u32[]{:S(2)}) async-start(bf16[32,2,128,128]{3,2,1,0:T(8,128)(2,1)} %copy-done), calls=%async_computation.1 | async-start | bytes 4194304 | tf_op jit(solution)/shard_map/all_to_all | solution.py:319
  187.2 3.5 %collective-permute-start.1 = (bf16[32,128,128]{2,1,0:T(8,128)(2,1)S(1)}, bf16[32,128,128]{2,1,0:T(8,128)(2,1)}, u32[]{:S(2)}, u32[]{:S(2)}) collective-permute-start(bf16[32,128,128]{2,1,0:T(8,128)(2,1)S(1)} %get-tuple-element.13), channel_id=1, source_target_pairs={{1,33},{3,35},{5,37},{7,39},{9,41},{11,43},{13,45},{15,47},{17,49}... | collective-permute-start | bytes 3145736 | tf_op jit(solution)/shard_map/ppermute | solution.py:301
  190.7 24.7 %all-to-all-done.1.rows_ref = bf16[32,2,128,128]{3,2,1,0:T(8,128)(2,1)S(1)} async-done(((bf16[32,2,128,128]{3,2,1,0:T(8,128)(2,1)}), bf16[32,2,128,128]{3,2,1,0:T(8,128)(2,1)S(1)}, u32[]{:S(2)}, u32[]{:S(2)}) %all-to-all-start.1) | async-done | bytes 2097184 | tf_op jit(solution)/shard_map/all_to_all | solution.py:319
  215.5 2.2 place_rows.1.before_ref
  217.6 1.6 collective-permute-start.2
  219.3 0.0 collective-permute-done.1.single_ref
  219.3 0.0 collective-permute-done.pair_ref
  219.3 2.3 stack_rows.1.in_ref
  221.6 4.6 %all-to-all-start.2 = ((bf16[32,2,128,128]{3,2,1,0:T(8,128)(2,1)}), bf16[32,2,128,128]{3,2,1,0:T(8,128)(2,1)}, u32[]{:S(2)}, u32[]{:S(2)}) async-start(bf16[32,2,128,128]{3,2,1,0:T(8,128)(2,1)} %rows_after.1), calls=%async_computation.2 | async-start | bytes 4194304 | tf_op jit(solution)/shard_map/all_to_all | solution.py:329
  226.1 28.1 %collective-permute-done.2.in_ref = bf16[256,3072]{1,0:T(8,128)(2,1)} collective-permute-done((bf16[256,3072]{1,0:T(8,128)(2,1)}, bf16[256,3072]{1,0:T(8,128)(2,1)}, u32[]{:S(2)}, u32[]{:S(2)}) %collective-permute-start.2) | collective-permute-done | bytes 1572896 | tf_op jit(solution)/shard_map/ppermute | solution.py:301
  254.2 0.0 all-to-all-done.2.rows_ref
  254.2 3.8 %join_rows.1 = bf16[512,3072]{1,0:T(8,128)(2,1)} custom-call(s32[40]{0:T(128)S(1)} %copy-done.2, bf16[32,2,128,128]{3,2,1,0:T(8,128)(2,1)} %all-to-all-done.2.rows_ref, bf16[256,3072]{1,0:T(8,128)(2,1)} %rows_shifted.1.done_ref), custom_call_target="tpu_custom_call" | custom-call | bytes 1000 | tf_op jit(solution)/shard_map/join_rows/pallas_call | solution.py:330
  (6 shorter events, 0.0 us)
Async XLA Ops:
  10.0 149.3 %copy-start.1 = (s32[24,128]{1,0:T(8,128)S(1)}, s32[24,128]{1,0:T(8,128)}, u32[]{:S(2)}) copy-start(s32[24,128]{1,0:T(8,128)} %counts_ref.3) | copy-start | bytes 36868
  10.0 149.3 %copy-start.2 = (s32[40]{0:T(128)S(1)}, s32[40]{0:T(128)}, u32[]{:S(2)}) copy-start(s32[40]{0:T(128)} %get-tuple-element.10.slot_ref) | copy-start | bytes 484
  10.1 149.3 %copy-start.3 = (bf16[1,3072]{1,0:T(2,128)(2,1)S(1)}, bf16[1,3072]{1,0:T(2,128)(2,1)}, u32[]{:S(2)}) copy-start(bf16[1,3072]{1,0:T(2,128)(2,1)} %gate_ref.1) | copy-start | bytes 18436
  10.1 149.3 %copy-start.4 = (s32[2,128,8]{1,2,0:T(8,128)S(1)}, s32[2,128,8]{1,2,0:T(8,128)}, u32[]{:S(2)}) copy-start(s32[2,128,8]{1,2,0:T(8,128)} %param.8) | copy-start | bytes 24580
  10.1 149.3 %copy-start.5 = (s32[24]{0:T(128)S(1)}, s32[24]{0:T(128)}, u32[]{:S(2)}) copy-start(s32[24]{0:T(128)} %class_ref.1) | copy-start | bytes 292
  173.2 1.3 copy-start
  174.5 44.8 %collective-permute-start = (bf16[32,2,128,128]{3,2,1,0:T(8,128)(2,1)}, bf16[32,2,128,128]{3,2,1,0:T(8,128)(2,1)}, u32[]{:S(2)}, u32[]{:S(2)}) collective-permute-start(bf16[32,2,128,128]{3,2,1,0:T(8,128)(2,1)} %get-tuple-element.12), channel_id=1, source_target_pairs={{0,32},{2,34},{4,36},{6,38},{8,40},{10,42},{12,44},{14,46},{16,48}... | collective-permute-start | bytes 6291464 | tf_op jit(solution)/shard_map/ppermute | solution.py:301
  176.5 39.0 %all-to-all-start.1 = ((bf16[32,2,128,128]{3,2,1,0:T(8,128)(2,1)}), bf16[32,2,128,128]{3,2,1,0:T(8,128)(2,1)S(1)}, u32[]{:S(2)}, u32[]{:S(2)}) async-start(bf16[32,2,128,128]{3,2,1,0:T(8,128)(2,1)} %copy-done), calls=%async_computation.1 | async-start | bytes 4194304 | tf_op jit(solution)/shard_map/all_to_all | solution.py:319
  187.2 32.1 %collective-permute-start.1 = (bf16[32,128,128]{2,1,0:T(8,128)(2,1)S(1)}, bf16[32,128,128]{2,1,0:T(8,128)(2,1)}, u32[]{:S(2)}, u32[]{:S(2)}) collective-permute-start(bf16[32,128,128]{2,1,0:T(8,128)(2,1)S(1)} %get-tuple-element.13), channel_id=1, source_target_pairs={{1,33},{3,35},{5,37},{7,39},{9,41},{11,43},{13,45},{15,47},{17,49}... | collective-permute-start | bytes 3145736 | tf_op jit(solution)/shard_map/ppermute | solution.py:301
  217.6 36.6 %collective-permute-start.2 = (bf16[256,3072]{1,0:T(8,128)(2,1)}, bf16[256,3072]{1,0:T(8,128)(2,1)}, u32[]{:S(2)}, u32[]{:S(2)}) collective-permute-start(bf16[256,3072]{1,0:T(8,128)(2,1)} %place_rows.1.before_ref), channel_id=1, source_target_pairs={{0,32},{1,33},{2,34},{3,35},{4,36},{5,37},{6,38},{7,39},{8,40},{9,... | collective-permute-start | bytes 4718600 | tf_op jit(solution)/shard_map/ppermute | solution.py:301
  221.6 32.7 %all-to-all-start.2 = ((bf16[32,2,128,128]{3,2,1,0:T(8,128)(2,1)}), bf16[32,2,128,128]{3,2,1,0:T(8,128)(2,1)}, u32[]{:S(2)}, u32[]{:S(2)}) async-start(bf16[32,2,128,128]{3,2,1,0:T(8,128)(2,1)} %rows_after.1), calls=%async_computation.2 | async-start | bytes 4194304 | tf_op jit(solution)/shard_map/all_to_all | solution.py:329
